TPU v7x, 512 devices: a whole 4x8x8 slice. The times are simulated.
512 devices in a mesh: tile: 256 (over z, y, x), depth: 2 (over core).
Axes of the slice: x: 4, y: 8, z: 8, core: 2. Of those that a mesh axis runs over, the one named last changes fastest.
Arguments:
- density: float32 [64, 4096, 256], P('depth', 'tile'), may hold values from -6 to 6
- absorption: float32 [4096, 256], P('tile'), may hold values from 0.25 to 32
- view_dir: int32 [4096], P('tile'), may hold values 0 or 1
- target_ids: int32 [4096, 256], P('tile'), may hold values from 0 to 127
- palette: float32 [3, 128], replicated, may hold values from -3 to 3
- emission_coef: float32 [3, 4], replicated, may hold values from -3 to 3
- light: float32 [3], replicated, may hold values from -4 to 4
Outputs:
- image: float32 [3, 4096, 256], P(None, ('tile', 'depth'))
- density_grad: float32 [64, 4096, 256], P('depth', 'tile')
All inputs are finite; a program needn't handle non-finite values. No bound on the sum of `view_dir` on one device may be relied on, other than what follows from the above.
Results may differ from a plain program's by a relative error of at most 0.00023.
Values sent between devices are 32-bit elements; how exact they have to be, the bound alone decides.
A program may use at most 64 MiB of HBM per device.

v0:
```python
import jax
import jax.numpy as jnp
from jax import lax
from jax.sharding import PartitionSpec as P


def extended(cells, sides, width):
    for axis, dim in sides:
        count = lax.axis_size(axis)
        ends = count - 1
        head = lax.slice_in_dim(cells, 0, width, axis=dim)
        tail = lax.slice_in_dim(cells, cells.shape[dim] - width, cells.shape[dim], axis=dim)
        cells = jnp.concatenate(
            [
                lax.ppermute(tail, axis, [(i, (i + 1) % count) for i in range(ends)]),
                cells,
                lax.ppermute(head, axis, [((i + 1) % count, i) for i in range(ends)]),
            ],
            axis=dim,
        )
    return cells


def entering(value, axis, combine, identity, reverse):
    length, here = (lax.axis_size(axis), lax.axis_index(axis))
    everything = jax.tree.map(lambda part: lax.all_gather(part, axis), value)
    start = jax.tree.map(
        lambda part, zero: jnp.broadcast_to(jnp.asarray(zero, part.dtype), part.shape),
        value,
        identity,
    )

    def step(k, before):
        at = length - 1 - k if reverse else k
        reached = at > here if reverse else at < here
        new = combine(before, jax.tree.map(lambda part: part[at], everything))
        return jax.tree.map(lambda a, b: jnp.where(reached, a, b), new, before)

    return lax.fori_loop(0, length, step, start)


def smooth_field(ext):
    core = ext[1:-1, 1:-1]
    total = 2.0 * core + ext[2:, 1:-1] + ext[:-2, 1:-1] + ext[1:-1, 2:] + ext[1:-1, :-2]
    total = total + jnp.roll(core, -1, 2) + jnp.roll(core, 1, 2)
    return total / 8.0


def shade_parts(padded, absorption, emission_coef, light, depth_count):
    smoothed = smooth_field(padded)
    centre = smoothed[1:-1, 1:-1]
    grad_z = 0.5 * (smoothed[2:, 1:-1] - smoothed[:-2, 1:-1])
    grad_y = 0.5 * (smoothed[1:-1, 2:] - smoothed[1:-1, :-2])
    grad_x = 0.5 * (jnp.roll(centre, -1, 2) - jnp.roll(centre, 1, 2))
    facing = grad_z * light[0] + grad_y * light[1] + grad_x * light[2]
    shade = 0.5 + 0.5 * facing / jnp.sqrt(1.0 + grad_z * grad_z + grad_y * grad_y + grad_x * grad_x)
    value = (
        emission_coef[:, 3][:, None, None, None] * centre[None]
        + emission_coef[:, 2][:, None, None, None]
    )
    value = value * centre[None] + emission_coef[:, 1][:, None, None, None]
    value = value * centre[None] + emission_coef[:, 0][:, None, None, None]
    emission = value * shade[None]
    sigma = absorption[None] * jax.nn.softplus(centre) / depth_count
    return (emission, sigma)


def compose(first, second):
    return (first[0] + jnp.exp(-first[1])[None] * second[0], first[1] + second[1])


def choose(mask, when_true, when_false):
    return (
        jnp.where(mask, when_true[0], when_false[0]),
        jnp.where(mask, when_true[1], when_false[1]),
    )


def lookup_target(target_ids, palette):
    rows, cols = target_ids.shape
    entries = palette.shape[1]
    onehot = (
        target_ids.reshape(1, rows * cols) == jnp.arange(entries, dtype=jnp.int32)[:, None]
    ).astype(jnp.float32)
    return jnp.dot(palette, onehot, precision=lax.Precision.HIGHEST).reshape(3, rows, cols)


def shards(density, absorption, view_dir, target_ids, palette, emission_coef, light):
    slab, rows, cols = density.shape
    depth_count = slab * lax.axis_size("depth")
    position = lax.axis_index("depth")
    share = rows // lax.axis_size("depth")
    flipped = (view_dir == 1)[:, None]
    flipped_cube = flipped[None]

    def combine_low(earlier, later):
        return compose(choose(flipped, later, earlier), choose(flipped, earlier, later))

    def combine_high(earlier, later):
        return compose(choose(flipped, earlier, later), choose(flipped, later, earlier))

    padded = extended(density, (("tile", 1), ("depth", 0)), 2)

    def local_render(field):
        emission, sigma = shade_parts(field, absorption, emission_coef, light, depth_count)
        ascending = jnp.cumsum(sigma, 0) - sigma
        total = jnp.sum(sigma, 0)
        descending = total[None] - ascending - sigma
        depth_before = jnp.where(flipped_cube, descending, ascending)
        weight = jnp.exp(-depth_before) * (1.0 - jnp.exp(-sigma))
        return (jnp.sum(emission * weight[None], 1), total)

    local_state, pullback = jax.vjp(local_render, padded)
    identity = (jnp.zeros_like(local_state[0]), jnp.zeros_like(local_state[1]))
    below = entering(local_state, "depth", combine_low, identity, False)
    above = entering(local_state, "depth", combine_high, identity, True)
    before = choose(flipped, above, below)
    after = choose(flipped, below, above)
    fade = jnp.exp(-before[1])[None]
    image = before[0] + fade * (local_state[0] + jnp.exp(-local_state[1])[None] * after[0])
    target = lookup_target(target_ids, palette)
    misfit = (image - target) * depth_count
    grad_colour = fade * misfit
    grad_depth = -(jnp.exp(-before[1] - local_state[1]) * jnp.sum(misfit * after[0], 0))
    (grad_ext,) = pullback((grad_colour, grad_depth))
    edges = jnp.concatenate([grad_ext[:2], grad_ext[-2:]], 0)
    arrived = extended(edges, (("depth", 0),), 2)
    inner = grad_ext[2:-2]
    inner = jnp.concatenate([inner[:2] + arrived[:2], inner[2:-2], inner[-2:] + arrived[-2:]], 0)
    sides = jnp.concatenate([inner[:, :2], inner[:, -2:]], 1)
    landed = extended(sides, (("tile", 1),), 2)
    middle = inner[:, 2:-2]
    density_grad = jnp.concatenate(
        [middle[:, :2] + landed[:, :2], middle[:, 2:-2], middle[:, -2:] + landed[:, -2:]], 1
    )
    image_rows = lax.dynamic_slice_in_dim(image, position * share, share, 1)
    return (image_rows, density_grad)


def solution(mesh):
    placed = (P("depth", "tile", None), P("tile", None), P("tile"), P("tile", None), P(), P(), P())
    return jax.shard_map(
        shards,
        mesh=mesh,
        in_specs=placed,
        out_specs=(P(None, ("tile", "depth"), None), P("depth", "tile", None)),
        check_vma=False,
    )
```

profile of v0, /device:TPU:254, one launch (start us, length us, event | category | flops | bytes accessed | tf_op | source)
XLA Modules:
  0.0 81.6 jit_solution(13606384222050139219)
XLA Ops:
  0.7 1.1 %fusion.64 = (f32[32,2,256]{2,1,0:T(2,128)S(1)}, f32[32,2,256]{2,1,0:T(2,128)S(1)}) fusion(f32[32,16,256]{2,1,0:T(8,128)} %param.11), kind=kLoop, calls=%fused_computation.142 | loop fusion | bytes 262144 | tf_op jit(solution)/shard_map/slice | solution.py:12
  1.8 4.6 %collective-permute-start = (f32[32,2,256]{2,1,0:T(2,128)S(1)}, f32[32,2,256]{2,1,0:T(2,128)S(1)}, u32[]{:S(2)}, u32[]{:S(2)}) collective-permute-start(f32[32,2,256]{2,1,0:T(2,128)S(1)} %get-tuple-element.439), channel_id=1, source_target_pairs={{0,2},{2,4},{4,6},{6,8},{8,10},{10,12},{12,14},{14,16},{16,18},{18... | collective-permute-start | bytes 196616 | tf_op jit(solution)/shard_map/ppermute | solution.py:15
  6.4 1.9 %collective-permute-start.1 = (f32[32,2,256]{2,1,0:T(2,128)S(1)}, f32[32,2,256]{2,1,0:T(2,128)S(1)}, u32[]{:S(2)}, u32[]{:S(2)}) collective-permute-start(f32[32,2,256]{2,1,0:T(2,128)S(1)} %get-tuple-element.440), channel_id=1, source_target_pairs={{2,0},{4,2},{6,4},{8,6},{10,8},{12,10},{14,12},{16,14},{18,16},{20... | collective-permute-start | bytes 196616 | tf_op jit(solution)/shard_map/ppermute | solution.py:17
  8.3 0.7 broadcast_compare_fusion
  9.0 0.7 copy.9
  9.7 1.3 %broadcast_multiply_fusion.2 = f32[16,256]{1,0:T(8,128)} fusion(f32[16,256]{1,0:T(8,128)} %param.12), kind=kLoop, calls=%fused_computation.120 | loop fusion | flops 4096 | bytes 32768 | tf_op jit(solution)/shard_map/transpose(jvp())/mul | solution.py:64
  11.1 1.4 %fusion.12 = f32[4096,3]{0,1:T(4,128)} fusion(f32[3,128]{1,0:T(4,128)S(1)} %copy-done, s32[4096]{0:T(1024)S(1)} %bitcast.87), kind=kOutput, calls=%fused_computation.25 | convolution fusion | flops 19398656 | bytes 67072 | tf_op jit(solution)/shard_map/dot_general | solution.py:85
  12.4 1.6 %slice_reduce_fusion.3 = (f32[3]{0:T(128)S(1)}, f32[3]{0:T(128)}, f32[3]{0:T(128)}, f32[3]{0:T(128)}) fusion(f32[3,4]{1,0:T(4,128)} %param.16), kind=kLoop, calls=%fused_computation.126 | loop fusion | bytes 96 | tf_op jit(solution)/shard_map/jvp()/slice | solution.py:58
  14.1 3.9 %collective-permute-done.1 = f32[32,2,256]{2,1,0:T(2,128)S(1)} collective-permute-done((f32[32,2,256]{2,1,0:T(2,128)S(1)}, f32[32,2,256]{2,1,0:T(2,128)S(1)}, u32[]{:S(2)}, u32[]{:S(2)}) %collective-permute-start.1) | collective-permute-done | bytes 65568 | tf_op jit(solution)/shard_map/ppermute | solution.py:17
  18.0 1.3 %collective-permute-start.2 = (f32[2,20,256]{2,1,0:T(8,128)S(1)}, f32[2,20,256]{2,1,0:T(8,128)S(1)}, u32[]{:S(2)}, u32[]{:S(2)}) collective-permute-start(f32[2,20,256]{2,1,0:T(8,128)S(1)} %get-tuple-element.437), channel_id=1, source_target_pairs={{0,1},{2,3},{4,5},{6,7},{8,9},{10,11},{12,13},{14,15},{16,17},{18,... | collective-permute-start | bytes 122888 | tf_op jit(solution)/shard_map/ppermute | solution.py:15
  19.3 1.3 %collective-permute-start.3 = (f32[2,20,256]{2,1,0:T(8,128)S(1)}, f32[2,20,256]{2,1,0:T(8,128)S(1)}, u32[]{:S(2)}, u32[]{:S(2)}) collective-permute-start(f32[2,20,256]{2,1,0:T(8,128)S(1)} %get-tuple-element.438), channel_id=1, source_target_pairs={{1,0},{3,2},{5,4},{7,6},{9,8},{11,10},{13,12},{15,14},{17,16},{19,... | collective-permute-start | bytes 122888 | tf_op jit(solution)/shard_map/ppermute | solution.py:17
  20.6 0.7 fusion.65
  23.9 0.7 fusion.24
  25.4 1.6 %divide_add_fusion = (f32[32,16,256]{2,1,0:T(8,128)S(1)}, f32[32,16,256]{2,1,0:T(8,128)S(1)}, f32[32,16,256]{2,1,0:T(8,128)}, f32[32,16,256]{2,1,0:T(8,128)}, f3...) fusion(f32[34,18,256]{2,1,0:T(8,128)S(1)} %fusion.24, f32[]{:T(128)} %bitcast.3, f32[]{:T(128)} %bitcast.2, f32[]{:T(128)} %bitcast.1, ...), kind=kLoop, calls=%fused_computation.91 | loop fusion | flops 4059136 | bytes 6324236 | tf_op jit(solution)/shard_map/jvp()/add | solution.py:56
  27.0 0.6 negate_exponential_fusion.5
  27.7 2.6 %all-gather.1 = f32[32,256]{1,0:T(8,128)S(1)} all-gather(f32[16,256]{1,0:T(8,128)S(1)} %get-tuple-element.430), channel_id=3, replica_groups=mesh['tile'=256,'depth'=2] {'depth'}, dimensions={0}, use_global_device_ids=true | all-gather | bytes 49152 | tf_op jit(solution)/shard_map/all_gather | solution.py:26
  30.3 0.6 subtract_multiply_fusion
  31.5 0.6 copy-done.8
  32.1 2.2 %all-gather = f32[6,16,256]{2,1,0:T(8,128)} all-gather(f32[3,16,256]{2,1,0:T(8,128)S(1)} %multiply_reduce_fusion.1), channel_id=2, replica_groups=mesh['tile'=256,'depth'=2] {'depth'}, dimensions={0}, use_global_device_ids=true | all-gather | bytes 147456 | tf_op jit(solution)/shard_map/all_gather | solution.py:26
  34.3 5.1 %while.35 = (s32[]{:T(128)}, f32[3,16,256]{2,1,0:T(8,128)}, f32[16,256]{1,0:T(8,128)}, s32[]{:T(128)}, pred[16,1]{0,1:T(4,128)(4,1)S(1)}, /*index=5*/f32[2,3,16,...) while((s32[]{:T(128)}, f32[3,16,256]{2,1,0:T(8,128)}, f32[16,256]{1,0:T(8,128)}, ...), condition=%wide.region_6.7_spmd.clone, body=%wide.region_5.6_spmd.clone.sunk | while | flops 98308 | bytes 229539 | solution.py:39
  34.3 0.7 fusion.73
  35.0 1.5 %fusion.74 = f32[3,16,256]{2,1,0:T(8,128)} fusion(f32[3,16,256]{2,1,0:T(8,128)} %get-tuple-element.552, f32[2,3,16,256]{3,2,1,0:T(8,128)} %get-tuple-element.565, s32[]{:T(128)S(6)} %copy.19, f32[16,256]{1,0:T(8,128)S(1)} %get-tuple-element.540, pred[16]{0:T(512)(128)(4,1)S(1)} %bitcast.83, pred[]{:T(512)S(6)} %compare.25, pred[]{:T(512)S(6)} %lt.49), kind=kLoop, calls=%fused_computation.13.clone.1 | loop fusion | flops 73728 | bytes 163862 | tf_op jit(solution)/shard_map/while/body/eval_jaxpr/jit(_where)/select_n | solution.py:37
  36.4 1.4 %fusion.73 = (f32[16,256]{1,0:T(8,128)}, f32[16,256]{1,0:T(8,128)S(1)}) fusion(f32[16,256]{1,0:T(8,128)} %get-tuple-element.553, f32[2,16,256]{2,1,0:T(8,128)S(1)} %get-tuple-element.566, s32[]{:T(128)S(6)} %copy.19, pred[16]{0:T(512)(128)(4,1)S(1)} %bitcast.82, pred[]{:T(512)S(6)} %compare.25, pred[]{:T(512)S(6)} %lt.49), kind=kLoop, calls=%fused_computation.18.clone.1 | loop fusion | flops 24576 | bytes 65558 | tf_op jit(solution)/shard_map/while/body/eval_jaxpr/jit(_where)/select_n | solution.py:37
  37.8 1.5 %fusion.74 = f32[3,16,256]{2,1,0:T(8,128)} fusion(f32[3,16,256]{2,1,0:T(8,128)} %get-tuple-element.552, f32[2,3,16,256]{3,2,1,0:T(8,128)} %get-tuple-element.565, s32[]{:T(128)S(6)} %copy.19, f32[16,256]{1,0:T(8,128)S(1)} %get-tuple-element.540, pred[16]{0:T(512)(128)(4,1)S(1)} %bitcast.83, pred[]{:T(512)S(6)} %compare.25, pred[]{:T(512)S(6)} %lt.49), kind=kLoop, calls=%fused_computation.13.clone.1 | loop fusion | flops 73728 | bytes 163862 | tf_op jit(solution)/shard_map/while/body/eval_jaxpr/jit(_where)/select_n | solution.py:37
  39.4 3.9 %while.34 = (s32[]{:T(128)}, f32[3,16,256]{2,1,0:T(8,128)S(1)}, f32[16,256]{1,0:T(8,128)}, s32[]{:T(128)}, pred[16,1]{0,1:T(4,128)(4,1)S(1)}, /*index=5*/f32[2,3...) while((s32[]{:T(128)}, f32[3,16,256]{2,1,0:T(8,128)S(1)}, ...), condition=%wide.region_4.5_spmd.clone, body=%wide.region_3.4_spmd.clone.sunk | while | flops 98312 | bytes 229593 | solution.py:39
  39.4 0.7 fusion.71
  40.0 0.9 %fusion.72 = f32[3,16,256]{2,1,0:T(8,128)S(1)} fusion(f32[3,16,256]{2,1,0:T(8,128)S(1)} %get-tuple-element.580, f32[2,3,16,256]{3,2,1,0:T(8,128)} %get-tuple-element.594, s32[]{:T(128)S(6)} %select_n.362, f32[16,256]{1,0:T(8,128)S(1)} %get-tuple-element.531, pred[16]{0:T(512)(128)(4,1)S(1)} %bitcast.85, pred[]{:T(512)S(6)} %compare.24, pred[]{:T(512)S(6)} %gt.12), kind=kLoop, calls=%fused_computation.3.clone.1 | loop fusion | flops 73728 | bytes 163862 | tf_op jit(solution)/shard_map/while/body/eval_jaxpr/jit(_where)/select_n | solution.py:37
  41.0 1.4 %fusion.71 = (f32[16,256]{1,0:T(8,128)}, f32[16,256]{1,0:T(8,128)S(1)}) fusion(f32[16,256]{1,0:T(8,128)} %get-tuple-element.581, f32[2,16,256]{2,1,0:T(8,128)S(1)} %get-tuple-element.595, s32[]{:T(128)S(6)} %select_n.362, pred[16]{0:T(512)(128)(4,1)S(1)} %bitcast.84, pred[]{:T(512)S(6)} %compare.24, pred[]{:T(512)S(6)} %gt.12), kind=kLoop, calls=%fused_computation.8.clone.1 | loop fusion | flops 24576 | bytes 65558 | tf_op jit(solution)/shard_map/while/body/eval_jaxpr/jit(_where)/select_n | solution.py:37
  42.4 0.9 %fusion.72 = f32[3,16,256]{2,1,0:T(8,128)S(1)} fusion(f32[3,16,256]{2,1,0:T(8,128)S(1)} %get-tuple-element.580, f32[2,3,16,256]{3,2,1,0:T(8,128)} %get-tuple-element.594, s32[]{:T(128)S(6)} %select_n.362, f32[16,256]{1,0:T(8,128)S(1)} %get-tuple-element.531, pred[16]{0:T(512)(128)(4,1)S(1)} %bitcast.85, pred[]{:T(512)S(6)} %compare.24, pred[]{:T(512)S(6)} %gt.12), kind=kLoop, calls=%fused_computation.3.clone.1 | loop fusion | flops 73728 | bytes 163862 | tf_op jit(solution)/shard_map/while/body/eval_jaxpr/jit(_where)/select_n | solution.py:37
  43.2 0.8 broadcast_multiply_fusion.3
  44.1 1.0 %multiply_reduce_fusion.2 = (f32[16,256]{1,0:T(8,128)S(1)}, f32[3,16,256]{2,1,0:T(8,128)S(1)}) fusion(f32[3,16,256]{2,1,0:T(8,128)} %get-tuple-element.305, f32[3,16,256]{2,1,0:T(8,128)S(1)} %get-tuple-element.304, pred[16]{0:T(512)(128)(4,1)S(1)} %get-tuple-element.444, f32[1,3,16,256]{3,1,2,0:T(4,128)} %bitcast.80, f32[3,16,256]{2,1,0:T(8,128)} %copy-done.8, ...), kind=kLoop, calls=%fused_computation.113 | loop fusion | flops 118784 | bytes 294928 | tf_op jit(solution)/shard_map/reduce_sum | solution.py:124
  45.0 0.6 copy-done.11
  45.6 0.9 %broadcast_multiply_fusion.1 = f32[3,16,256]{2,1,0:T(8,128)S(1)} fusion(f32[16,256]{1,0:T(8,128)S(1)} %get-tuple-element.408, f32[3,16,256]{2,1,0:T(8,128)S(1)} %get-tuple-element.407, f32[1,3,16,256]{3,1,2,0:T(4,128)} %bitcast.81), kind=kLoop, calls=%fused_computation.115 | loop fusion | flops 24576 | bytes 163840 | tf_op jit(solution)/shard_map/mul | solution.py:123
  46.5 2.3 %fusion.18 = (f32[32,16,256]{2,1,0:T(8,128)S(1)}, f32[32,16,256]{2,1,0:T(8,128)S(1)}, f32[32,16,256]{2,1,0:T(8,128)S(1)}, f32[32,16,256]{2,1,0:T(8,128)S(1)}, f32[32,16,256]{2,1,0:T(8,128)S(1)}) fusion(f32[3,16,256]{2,1,0:T(8,128)S(1)} %broadcast_multiply_fusion.1, f32[32,16,256]{2,1,0:T(8,128)S(1)} %get-tuple-element.446, ...), kind=kLoop, calls=%fused_computation.31 | loop fusion | flops 7602176 | bytes 4243504 | tf_op jit(solution)/shard_map/transpose(jvp())/reduce_sum | solution.py:62
  49.1 0.7 copy-done.2
  49.8 0.8 fusion.53
  51.5 1.5 %fusion.27 = f32[32,16,256]{2,1,0:T(8,128)S(1)} fusion(f32[32,16,256]{2,1,0:T(8,128)S(1)} %get-tuple-element.447, f32[32,16,256]{2,1,0:T(8,128)S(1)} %get-tuple-element.360, f32[16,256]{1,0:T(8,128)S(1)} %copy-done.13, f32[16,256]{1,0:T(8,128)S(1)} %negate_add_fusion, pred[16]{0:T(512)(128)(4,1)S(1)} %get-tuple-element.444, f32[34,18,256]{2,1,0:T(8,128)S(1)} %fusion.24, ...), kind=kOutput, calls=%fused_computation.64 | output fusion | flops 9830400 | bytes 3736576 | tf_op jit(solution)/shard_map/transpose(jvp(jit(cumsum)))/reduce_window_sum | solution.py:106
  52.9 0.7 fusion.35
  55.0 2.2 %collective-permute-start.4 = (f32[2,20,256]{2,1,0:T(8,128)S(1)}, f32[2,20,256]{2,1,0:T(8,128)S(1)}, u32[]{:S(2)}, u32[]{:S(2)}) collective-permute-start(f32[2,20,256]{2,1,0:T(8,128)S(1)} %get-tuple-element.395), channel_id=1, source_target_pairs={{0,1},{2,3},{4,5},{6,7},{8,9},{10,11},{12,13},{14,15},{16,17},{18,... | collective-permute-start | bytes 122888 | tf_op jit(solution)/shard_map/ppermute | solution.py:15
  57.3 0.9 %collective-permute-done.4 = f32[2,20,256]{2,1,0:T(8,128)S(1)} collective-permute-done((f32[2,20,256]{2,1,0:T(8,128)S(1)}, f32[2,20,256]{2,1,0:T(8,128)S(1)}, u32[]{:S(2)}, u32[]{:S(2)}) %collective-permute-start.4) | collective-permute-done | bytes 40992 | tf_op jit(solution)/shard_map/ppermute | solution.py:15
  58.2 1.3 %collective-permute-start.5 = (f32[2,20,256]{2,1,0:T(8,128)S(1)}, f32[2,20,256]{2,1,0:T(8,128)S(1)}, u32[]{:S(2)}, u32[]{:S(2)}) collective-permute-start(f32[2,20,256]{2,1,0:T(8,128)S(1)} %pad_add_fusion.2), channel_id=1, source_target_pairs={{1,0},{3,2},{5,4},{7,6},{9,8},{11,10},{13,12},{15,14},{17,16},{19,... | collective-permute-start | bytes 122888 | tf_op jit(solution)/shard_map/ppermute | solution.py:17
  59.8 1.5 %collective-permute-done.5 = f32[2,20,256]{2,1,0:T(8,128)S(1)} collective-permute-done((f32[2,20,256]{2,1,0:T(8,128)S(1)}, f32[2,20,256]{2,1,0:T(8,128)S(1)}, u32[]{:S(2)}, u32[]{:S(2)}) %collective-permute-start.5) | collective-permute-done | bytes 40992 | tf_op jit(solution)/shard_map/ppermute | solution.py:17
  61.4 5.4 %collective-permute-start.6 = (f32[32,2,256]{2,1,0:T(2,128)S(1)}, f32[32,2,256]{2,1,0:T(2,128)S(1)}, u32[]{:S(2)}, u32[]{:S(2)}) collective-permute-start(f32[32,2,256]{2,1,0:T(2,128)S(1)} %pad_maximum_fusion.10), channel_id=1, source_target_pairs={{0,2},{2,4},{4,6},{6,8},{8,10},{10,12},{12,14},{14,16},{16,18},{18... | collective-permute-start | bytes 196616 | tf_op jit(solution)/shard_map/ppermute | solution.py:15
  66.8 0.6 constant_dynamic-slice_fusion
  67.4 1.3 %collective-permute-done.6 = f32[32,2,256]{2,1,0:T(2,128)S(1)} collective-permute-done((f32[32,2,256]{2,1,0:T(2,128)S(1)}, f32[32,2,256]{2,1,0:T(2,128)S(1)}, u32[]{:S(2)}, u32[]{:S(2)}) %collective-permute-start.6) | collective-permute-done | bytes 65568 | tf_op jit(solution)/shard_map/ppermute | solution.py:15
  68.7 1.9 %collective-permute-start.7 = (f32[32,2,256]{2,1,0:T(2,128)S(1)}, f32[32,2,256]{2,1,0:T(2,128)S(1)}, u32[]{:S(2)}, u32[]{:S(2)}) collective-permute-start(f32[32,2,256]{2,1,0:T(2,128)S(1)} %get-tuple-element.436), channel_id=1, source_target_pairs={{2,0},{4,2},{6,4},{8,6},{10,8},{12,10},{14,12},{16,14},{18,16},{20... | collective-permute-start | bytes 196616 | tf_op jit(solution)/shard_map/ppermute | solution.py:17
  70.8 9.9 %collective-permute-done.7 = f32[32,2,256]{2,1,0:T(2,128)S(1)} collective-permute-done((f32[32,2,256]{2,1,0:T(2,128)S(1)}, f32[32,2,256]{2,1,0:T(2,128)S(1)}, u32[]{:S(2)}, u32[]{:S(2)}) %collective-permute-start.7) | collective-permute-done | bytes 65568 | tf_op jit(solution)/shard_map/ppermute | solution.py:17
  80.7 0.9 %pad_maximum_fusion.8 = f32[32,16,256]{2,1,0:T(8,128)} fusion(f32[32,2,256]{2,1,0:T(2,128)S(1)} %maximum_add_fusion, f32[32,12,256]{2,1,0:T(8,128)S(1)} %slice.199, f32[32,2,256]{2,1,0:T(2,128)S(1)} %get-tuple-element.435), kind=kLoop, calls=%fused_computation.76 | loop fusion | flops 262144 | bytes 1048576 | tf_op jit(solution)/shard_map/concatenate | solution.py:133
  (67 shorter events, 5.3 us)
Async XLA Ops:
  0.6 10.4 %copy-start = (f32[3,128]{1,0:T(4,128)S(1)}, f32[3,128]{1,0:T(4,128)}, u32[]{:S(2)}) copy-start(f32[3,128]{1,0:T(4,128)} %param.15) | copy-start | bytes 4612
  0.6 17.4 %copy-start.1 = (f32[32,16,256]{2,1,0:T(8,128)S(1)}, f32[32,16,256]{2,1,0:T(8,128)}, u32[]{:S(2)}) copy-start(f32[32,16,256]{2,1,0:T(8,128)} %param.11) | copy-start | bytes 1572868
  0.7 20.0 %copy-start.14 = (f32[3]{0:T(128)S(1)}, f32[3]{0:T(128)}, u32[]{:S(2)}) copy-start(f32[3]{0:T(128)} %param.17) | copy-start | bytes 40
  1.8 12.3 %collective-permute-start = (f32[32,2,256]{2,1,0:T(2,128)S(1)}, f32[32,2,256]{2,1,0:T(2,128)S(1)}, u32[]{:S(2)}, u32[]{:S(2)}) collective-permute-start(f32[32,2,256]{2,1,0:T(2,128)S(1)} %get-tuple-element.439), channel_id=1, source_target_pairs={{0,2},{2,4},{4,6},{6,8},{8,10},{10,12},{12,14},{14,16},{16,18},{18... | collective-permute-start | bytes 196616 | tf_op jit(solution)/shard_map/ppermute | solution.py:15
  6.4 11.6 %collective-permute-start.1 = (f32[32,2,256]{2,1,0:T(2,128)S(1)}, f32[32,2,256]{2,1,0:T(2,128)S(1)}, u32[]{:S(2)}, u32[]{:S(2)}) collective-permute-start(f32[32,2,256]{2,1,0:T(2,128)S(1)} %get-tuple-element.440), channel_id=1, source_target_pairs={{2,0},{4,2},{6,4},{8,6},{10,8},{12,10},{14,12},{16,14},{18,16},{20... | collective-permute-start | bytes 196616 | tf_op jit(solution)/shard_map/ppermute | solution.py:17
  18.0 5.3 %collective-permute-start.2 = (f32[2,20,256]{2,1,0:T(8,128)S(1)}, f32[2,20,256]{2,1,0:T(8,128)S(1)}, u32[]{:S(2)}, u32[]{:S(2)}) collective-permute-start(f32[2,20,256]{2,1,0:T(8,128)S(1)} %get-tuple-element.437), channel_id=1, source_target_pairs={{0,1},{2,3},{4,5},{6,7},{8,9},{10,11},{12,13},{14,15},{16,17},{18,... | collective-permute-start | bytes 122888 | tf_op jit(solution)/shard_map/ppermute | solution.py:15
  19.3 4.0 %collective-permute-start.3 = (f32[2,20,256]{2,1,0:T(8,128)S(1)}, f32[2,20,256]{2,1,0:T(8,128)S(1)}, u32[]{:S(2)}, u32[]{:S(2)}) collective-permute-start(f32[2,20,256]{2,1,0:T(8,128)S(1)} %get-tuple-element.438), channel_id=1, source_target_pairs={{1,0},{3,2},{5,4},{7,6},{9,8},{11,10},{13,12},{15,14},{17,16},{19,... | collective-permute-start | bytes 122888 | tf_op jit(solution)/shard_map/ppermute | solution.py:17
  24.7 0.7 copy-start.4
  27.0 3.8 %copy-start.9 = (f32[16,256]{1,0:T(8,128)}, f32[16,256]{1,0:T(8,128)S(1)}, u32[]{:S(2)}) copy-start(f32[16,256]{1,0:T(8,128)S(1)} %get-tuple-element.430) | copy-start | bytes 49156
  30.3 0.6 copy-start.15
  30.3 0.6 copy-start.16
  30.3 0.7 copy-start.17
  31.5 0.6 copy-start.8
  45.0 0.6 copy-start.11
  46.5 2.3 %copy-start.3 = (f32[32,16,256]{2,1,0:T(8,128)S(1)}, f32[32,16,256]{2,1,0:T(8,128)}, u32[]{:S(2)}) copy-start(f32[32,16,256]{2,1,0:T(8,128)} %get-tuple-element.412) | copy-start | bytes 1572868
  48.8 1.0 %copy-start.2 = (f32[32,16,256]{2,1,0:T(8,128)S(1)}, f32[32,16,256]{2,1,0:T(8,128)}, u32[]{:S(2)}) copy-start(f32[32,16,256]{2,1,0:T(8,128)} %get-tuple-element.413) | copy-start | bytes 1572868
  48.8 1.0 %copy-start.5 = (f32[16,256]{1,0:T(8,128)S(1)}, f32[16,256]{1,0:T(8,128)}, u32[]{:S(2)}) copy-start(f32[16,256]{1,0:T(8,128)} %param.12) | copy-start | bytes 49156
  50.6 0.7 copy-start.6
  50.6 0.7 copy-start.7
  50.7 0.7 copy-start.10
  50.7 0.8 copy-start.13
  55.0 3.1 %collective-permute-start.4 = (f32[2,20,256]{2,1,0:T(8,128)S(1)}, f32[2,20,256]{2,1,0:T(8,128)S(1)}, u32[]{:S(2)}, u32[]{:S(2)}) collective-permute-start(f32[2,20,256]{2,1,0:T(8,128)S(1)} %get-tuple-element.395), channel_id=1, source_target_pairs={{0,1},{2,3},{4,5},{6,7},{8,9},{10,11},{12,13},{14,15},{16,17},{18,... | collective-permute-start | bytes 122888 | tf_op jit(solution)/shard_map/ppermute | solution.py:15
  58.2 3.1 %collective-permute-start.5 = (f32[2,20,256]{2,1,0:T(8,128)S(1)}, f32[2,20,256]{2,1,0:T(8,128)S(1)}, u32[]{:S(2)}, u32[]{:S(2)}) collective-permute-start(f32[2,20,256]{2,1,0:T(8,128)S(1)} %pad_add_fusion.2), channel_id=1, source_target_pairs={{1,0},{3,2},{5,4},{7,6},{9,8},{11,10},{13,12},{15,14},{17,16},{19,... | collective-permute-start | bytes 122888 | tf_op jit(solution)/shard_map/ppermute | solution.py:17
  61.3 5.5 %copy-start.12 = (f32[3,16,256]{2,1,0:T(8,128)S(1)}, f32[3,16,256]{2,1,0:T(8,128)}, u32[]{:S(2)}) copy-start(f32[3,16,256]{2,1,0:T(8,128)} %copy-done.11) | copy-start | bytes 147460
  61.4 7.3 %collective-permute-start.6 = (f32[32,2,256]{2,1,0:T(2,128)S(1)}, f32[32,2,256]{2,1,0:T(2,128)S(1)}, u32[]{:S(2)}, u32[]{:S(2)}) collective-permute-start(f32[32,2,256]{2,1,0:T(2,128)S(1)} %pad_maximum_fusion.10), channel_id=1, source_target_pairs={{0,2},{2,4},{4,6},{6,8},{8,10},{10,12},{12,14},{14,16},{16,18},{18... | collective-permute-start | bytes 196616 | tf_op jit(solution)/shard_map/ppermute | solution.py:15
  68.7 11.9 %collective-permute-start.7 = (f32[32,2,256]{2,1,0:T(2,128)S(1)}, f32[32,2,256]{2,1,0:T(2,128)S(1)}, u32[]{:S(2)}, u32[]{:S(2)}) collective-permute-start(f32[32,2,256]{2,1,0:T(2,128)S(1)} %get-tuple-element.436), channel_id=1, source_target_pairs={{2,0},{4,2},{6,4},{8,6},{10,8},{12,10},{14,12},{16,14},{18,16},{20... | collective-permute-start | bytes 196616 | tf_op jit(solution)/shard_map/ppermute | solution.py:17
where the time goes:
time: 82.9 us; the launch traced here: 81.6 us
  other arithmetic  25.6 us (31%)
  starting transfers between devices  20 us (24%)
  waiting for transfers between devices  17.4 us (21%)
  local copies, waits for them, and re-layouts  9.41 us (11%)
  blocking collectives  4.78 us (6%)
  between operations  3.04 us (4%)
  matrix products  1.36 us (2%)
    ppermute x4, waiting for transfers between devices, extended(): lax.ppermute(head, axis, [((i + 1) % count, i) for i in range(ends)])  15.3 us
    ppermute x4, starting transfers between devices, extended(): lax.ppermute(tail, axis, [(i, (i + 1) % count) for i in range(ends)])  13.6 us
    select_n x8, other arithmetic, step(): return jax.tree.map(lambda a, b: jnp.where(reached, a, b), new, before)  8.93 us
    ppermute x4, starting transfers between devices, extended(): lax.ppermute(head, axis, [((i + 1) % count, i) for i in range(ends)])  6.43 us
    all_gather x2, blocking collectives, entering(): everything = jax.tree.map(lambda part: lax.all_gather(part, axis), value)  4.78 us
    unnamed x37, local copies, waits for them, and re-layouts  3.61 us
    reduce_sum x1, other arithmetic, shade_parts(): value = value * centre[None] + emission_coef[:, 0][:, None, None, None]  2.25 us
    ppermute x4, waiting for transfers between devices, extended(): lax.ppermute(tail, axis, [(i, (i + 1) % count) for i in range(ends)])  2.12 us
  transfers between devices with their start and end apart: 8, of which 5 were waited for; matrix products, arithmetic and copies ran while one was open for 9% of the time, Pallas kernels for 0%

commit v1 on v0

v1 whole, which is shorter than its diff:
```python
import functools
import math

import jax
import jax.numpy as jnp
from jax import lax
from jax.experimental import pallas as pl
from jax.experimental.pallas import tpu as pltpu
from jax.sharding import PartitionSpec as P

MESH = pl.DeviceIdType.MESH
LOG2E = math.log2(math.e)
CHUNKS = 4


def body(
    tiles, slab, rows, cols, depth_count,
    density, absorption, view_dir, target_ids, palette, coef, light,
    image_out, grad_out,
    field, smooth, shade_b, cz_b, cy_b, cx_b, fac_b, edge_b, ay_b, qz_b, full_b, grad_b,
    ab_v, ids_v, pal_v, view_s, coef_s, light_s, image_v, mine, theirs, tgt_v,
    back_y, back_z, back_d,
    load_sem, small_sem, halo_send, halo_recv, face_send, face_recv, mid_send, mid_recv,
    ret_send, ret_recv, out_sem,
):
    tile = lax.axis_index("tile")
    core = lax.axis_index("depth")
    other = 1 - core
    has_prev = tile > 0
    has_next = tile < tiles - 1
    ext = rows + 8
    step = slab // CHUNKS
    sign = 2 * core - 1
    first = (1 - core) * (slab - 1)

    def layer(k):
        return first + sign * k

    def chunk_start(i):
        return core * (step * i) + other * (slab - step - step * i)

    prev_id = (jnp.maximum(tile - 1, 0), core)
    next_id = (jnp.minimum(tile + 1, tiles - 1), core)
    across_id = (tile, other)
    prev_across = (jnp.maximum(tile - 1, 0), other)
    next_across = (jnp.minimum(tile + 1, tiles - 1), other)

    def rx(value, shift):
        return pltpu.roll(value, shift % cols, 1)

    def ry(value, shift):
        return pltpu.roll(value, shift % ext, 0)

    own = pltpu.make_async_copy(density, field.at[pl.ds(2, slab), pl.ds(0, rows), :], load_sem)
    own.start()
    smalls = [
        pltpu.make_async_copy(src, dst, small_sem.at[n])
        for n, (src, dst) in enumerate(
            [(view_dir, view_s), (absorption, ab_v), (light, light_s), (coef, coef_s), (target_ids, ids_v), (palette, pal_v)]
        )
    ]
    for copy in smalls:
        copy.start()

    zero_layer = jnp.zeros((ext, cols), jnp.float32)
    back_d[0] = jnp.zeros((8, cols), jnp.float32)

    field[2 + layer(slab)] = zero_layer

    @pl.when(jnp.logical_not(has_prev))
    def _():
        def clear(j, carry):
            field[j, pl.ds(rows + 6, 2), :] = jnp.zeros((2, cols), jnp.float32)
            return carry

        lax.fori_loop(0, slab + 4, clear, 0)

        def clear_back(j, carry):
            back_y[j, pl.ds(0, 2), :] = jnp.zeros((2, cols), jnp.float32)
            return carry

        lax.fori_loop(0, slab, clear_back, 0)

    @pl.when(jnp.logical_not(has_next))
    def _():
        def clear(j, carry):
            field[j, pl.ds(rows, 2), :] = jnp.zeros((2, cols), jnp.float32)
            return carry

        lax.fori_loop(0, slab + 4, clear, 0)

        def clear_back(j, carry):
            back_y[j, pl.ds(6, 2), :] = jnp.zeros((2, cols), jnp.float32)
            return carry

        lax.fori_loop(0, slab, clear_back, 0)

    barrier = pltpu.get_barrier_semaphore()
    pl.semaphore_signal(barrier, inc=1, device_id=across_id, device_id_type=MESH)

    @pl.when(has_prev)
    def _():
        pl.semaphore_signal(barrier, inc=1, device_id=prev_id, device_id_type=MESH)
        pl.semaphore_signal(barrier, inc=1, device_id=prev_across, device_id_type=MESH)

    @pl.when(has_next)
    def _():
        pl.semaphore_signal(barrier, inc=1, device_id=next_id, device_id_type=MESH)
        pl.semaphore_signal(barrier, inc=1, device_id=next_across, device_id_type=MESH)

    pl.semaphore_wait(barrier, 1 + 2 * has_prev.astype(jnp.int32) + 2 * has_next.astype(jnp.int32))

    face = pltpu.make_async_remote_copy(
        density.at[pl.ds(other * (slab - 2), 2)],
        field.at[pl.ds(core * (slab + 2), 2), pl.ds(0, rows), :],
        face_send.at[0], face_recv.at[0], device_id=across_id, device_id_type=MESH,
    )
    face_z = other * (slab - 1)
    face_at = 2 + core * slab - other
    corner_prev = pltpu.make_async_remote_copy(
        density.at[pl.ds(face_z, 1), pl.ds(0, 1), :],
        field.at[pl.ds(face_at, 1), pl.ds(rows, 1), :],
        face_send.at[1], face_recv.at[1], device_id=prev_across, device_id_type=MESH,
    )
    corner_next = pltpu.make_async_remote_copy(
        density.at[pl.ds(face_z, 1), pl.ds(rows - 1, 1), :],
        field.at[pl.ds(face_at, 1), pl.ds(rows + 7, 1), :],
        face_send.at[2], face_recv.at[2], device_id=next_across, device_id_type=MESH,
    )

    def halo_prev(i):
        start = chunk_start(i)
        return pltpu.make_async_remote_copy(
            density.at[pl.ds(start, step), pl.ds(0, 2), :],
            field.at[pl.ds(2 + start, step), pl.ds(rows, 2), :],
            halo_send.at[0, i], halo_recv.at[0, i], device_id=prev_id, device_id_type=MESH,
        )

    def halo_next(i):
        start = chunk_start(i)
        return pltpu.make_async_remote_copy(
            density.at[pl.ds(start, step), pl.ds(rows - 2, 2), :],
            field.at[pl.ds(2 + start, step), pl.ds(rows + 6, 2), :],
            halo_send.at[1, i], halo_recv.at[1, i], device_id=next_id, device_id_type=MESH,
        )

    face.start()

    @pl.when(has_prev)
    def _():
        corner_prev.start()

    @pl.when(has_next)
    def _():
        corner_next.start()

    for i in range(CHUNKS):

        @pl.when(has_prev)
        def _(i=i):
            halo_prev(i).start()

        @pl.when(has_next)
        def _(i=i):
            halo_next(i).start()

    for copy in smalls:
        copy.wait()
    row_of = lax.broadcasted_iota(jnp.int32, (rows, cols), 0)
    view = jnp.zeros((rows, cols), jnp.int32)
    for y in range(rows):
        view = jnp.where(row_of == y, view_s[y], view)
    ascending = view == other
    absorb = ab_v[...]
    half_light = [0.5 * light_s[0] * sign.astype(jnp.float32), 0.5 * light_s[1], 0.5 * light_s[2]]
    for c in range(3):
        table = jnp.broadcast_to(pal_v[pl.ds(c, 1), :], (8, pal_v.shape[1]))
        for y in range(0, rows, 8):
            for x in range(0, cols, 128):
                picked = jnp.take_along_axis(table, ids_v[pl.ds(y, 8), pl.ds(x, 128)], axis=1, mode="promise_in_bounds")
                tgt_v[c, pl.ds(y, 8), pl.ds(x, 128)] = picked

    own.wait()
    face.wait_recv()

    @pl.when(has_prev)
    def _():
        corner_next.wait_recv()

    @pl.when(has_next)
    def _():
        corner_prev.wait_recv()

    def blur(k):
        at = 2 + layer(k)
        here = field[at]
        total = 2.0 * here + field[at - 1] + field[at + 1]
        total = total + (ry(here, 1) + ry(here, -1)) + (rx(here, 1) + rx(here, -1))
        smooth[k + 1] = total

    scale = absorb * (LOG2E / depth_count)
    slope = absorb * (1.0 / (8.0 * depth_count))

    def shade(k, depth):
        here = smooth[k + 1]
        mid = here[:rows]
        dz = smooth[k + 2, pl.ds(0, rows), :] - smooth[k, pl.ds(0, rows), :]
        dy = ry(here, -1)[:rows] - ry(here, 1)[:rows]
        dx = rx(mid, -1) - rx(mid, 1)
        inv = lax.rsqrt(256.0 + dz * dz + dy * dy + dx * dx)
        facing = (half_light[0] * dz + half_light[1] * dy + half_light[2] * dx) * inv
        bend = facing * inv
        shade_b[k] = 0.5 + facing
        cz_b[k] = inv * (half_light[0] - bend * dz)
        cy_b[k] = inv * (half_light[1] - bend * dy)
        cx_b[k] = inv * (half_light[2] - bend * dx)
        power = mid * (LOG2E / 8.0)
        plus = jnp.log(1.0 + lax.exp2(power))
        fac_b[k] = slope * lax.exp2(power - plus * LOG2E)
        edge_b[k] = depth
        return depth + scale * plus

    def run(lo, count, unroll, one, carry):
        def several(j, carry):
            for u in range(unroll):
                carry = one(lo + j * unroll + u, carry)
            return carry

        return lax.fori_loop(0, count // unroll, several, carry)

    def blur_one(k, carry):
        blur(k)
        return carry

    depth = jnp.zeros((rows, cols), jnp.float32)
    for i in range(CHUNKS):

        @pl.when(has_prev)
        def _(i=i):
            halo_next(i).wait_recv()

        @pl.when(has_next)
        def _(i=i):
            halo_prev(i).wait_recv()

        run(step * i - 1, step, 2, blur_one, 0)
        if i:
            depth = run(step * (i - 1), step, 2, shade, depth)
    blur(slab - 1)
    smooth[slab + 1] = field[2 + layer(slab - 1)]
    depth = run(slab - step, step, 2, shade, depth)

    toward = jnp.where(ascending, -1.0, 1.0)
    base = jnp.where(ascending, 0.0, -depth)

    def composite(k, carry):
        left, m0, m1, m2, m3 = carry
        right = lax.exp2(toward * edge_b[k + 1] + base)
        mid = smooth[k + 1, pl.ds(0, rows), :]
        part = jnp.abs(left - right) * shade_b[k]
        m0 = m0 + part
        part = part * mid
        m1 = m1 + part
        part = part * mid
        m2 = m2 + part
        part = part * mid
        m3 = m3 + part
        edge_b[k] = left
        return (right, m0, m1, m2, m3)

    edge_b[slab] = depth
    zero = jnp.zeros((rows, cols), jnp.float32)
    left = lax.exp2(base)
    right, m0, m1, m2, m3 = run(0, slab, 2, composite, (left, zero, zero, zero, zero))
    edge_b[slab] = right
    for c in range(3):
        mine[c] = coef_s[c, 0] * m0 + (coef_s[c, 1] / 8.0) * m1 + (coef_s[c, 2] / 64.0) * m2 + (coef_s[c, 3] / 512.0) * m3
    mine[3] = depth
    swap = pltpu.make_async_remote_copy(
        mine, theirs, mid_send, mid_recv, device_id=across_id, device_id_type=MESH
    )
    swap.start()
    swap.wait()

    enter = jnp.where(ascending, lax.exp2(-theirs[3]), 1.0)
    leave = lax.exp2(-depth)
    misfit = []
    before = jnp.zeros((rows, cols), jnp.float32)
    for c in range(3):
        colour = jnp.where(ascending, theirs[c] + enter * mine[c], mine[c] + leave * theirs[c])
        image_v[c] = colour
        gap = (colour - tgt_v[c]) * float(depth_count)
        misfit.append(gap)
        before = before + gap * jnp.where(ascending, mine[c], theirs[c])
    rest = jnp.where(ascending, enter, leave) * before
    share = rows // 2
    image_copy = pltpu.make_async_copy(
        image_v.at[:, pl.ds(pl.multiple_of(core * share, 8), share), :], image_out, out_sem.at[CHUNKS]
    )
    image_copy.start()
    ramp = [
        enter
        * (misfit[0] * coef_s[0, i] + misfit[1] * coef_s[1, i] + misfit[2] * coef_s[2, i])
        * (1.0 / 8.0**i)
        for i in range(4)
    ]
    ramp2 = 2.0 * ramp[2]
    ramp3 = 3.0 * ramp[3]
    blank = jnp.zeros((8, cols), jnp.float32)

    def pull(k, rest):
        left = edge_b[k]
        signed = left - edge_b[k + 1]
        weight = jnp.abs(signed)
        mid = smooth[k + 1, pl.ds(0, rows), :]
        lit = shade_b[k]
        value = ramp[0] + mid * (ramp[1] + mid * (ramp[2] + mid * ramp[3]))
        deriv = ramp[1] + mid * (ramp2 + mid * ramp3)
        shown = lit * value
        pulled = weight * value
        direct = weight * lit * deriv + (left * shown - rest) * fac_b[k]
        qx = pulled * cx_b[k]
        qy = jnp.concatenate([pulled * cy_b[k], blank], 0)
        direct = direct + rx(qx, 1) - rx(qx, -1)
        ay_b[k] = ry(qy, 1) - ry(qy, -1) + jnp.concatenate([direct, blank], 0)
        qz_b[k + 1] = pulled * cz_b[k]
        return rest - signed * shown

    def gather(k, carry):
        full_b[k + 2, pl.ds(0, rows), :] = ay_b[k, pl.ds(0, rows), :] + qz_b[k] - qz_b[k + 2]
        full_b[k + 2, pl.ds(rows, 8), :] = ay_b[k, pl.ds(rows, 8), :]
        return carry

    def spread(k, carry):
        here = full_b[k + 2]
        total = 2.0 * here + full_b[k + 1] + full_b[k + 3]
        total = total + (ry(here, 1) + ry(here, -1)) + (rx(here, 1) + rx(here, -1))
        grad_b[2 + layer(k)] = total
        return carry

    def back_prev(i):
        start = chunk_start(i)
        return pltpu.make_async_remote_copy(
            grad_b.at[pl.ds(2 + start, step), pl.ds(rows + 6, 2), :],
            back_y.at[pl.ds(start, step), pl.ds(6, 2), :],
            ret_send.at[0, i], ret_recv.at[0, i], device_id=prev_id, device_id_type=MESH,
        )

    def back_next(i):
        start = chunk_start(i)
        return pltpu.make_async_remote_copy(
            grad_b.at[pl.ds(2 + start, step), pl.ds(rows, 2), :],
            back_y.at[pl.ds(start, step), pl.ds(0, 2), :],
            ret_send.at[1, i], ret_recv.at[1, i], device_id=next_id, device_id_type=MESH,
        )

    back_face = pltpu.make_async_remote_copy(
        grad_b.at[pl.ds(other * (slab + 2), 2), pl.ds(0, rows), :],
        back_z,
        face_send.at[3], face_recv.at[3], device_id=across_id, device_id_type=MESH,
    )
    back_corner_prev = pltpu.make_async_remote_copy(
        grad_b.at[face_ext(core, slab), pl.ds(rows + 7, 1), :],
        back_d.at[:, pl.ds(7, 1), :],
        face_send.at[4], face_recv.at[4], device_id=prev_across, device_id_type=MESH,
    )
    back_corner_next = pltpu.make_async_remote_copy(
        grad_b.at[face_ext(core, slab), pl.ds(rows, 1), :],
        back_d.at[:, pl.ds(0, 1), :],
        face_send.at[5], face_recv.at[5], device_id=next_across, device_id_type=MESH,
    )

    def send_back(i):
        @pl.when(has_prev)
        def _():
            back_prev(i).start()

        @pl.when(has_next)
        def _():
            back_next(i).start()

    qz_b[0] = zero
    qz_b[slab + 1] = zero
    for i in range(CHUNKS):
        rest = run(step * i, step, 2, pull, rest)
        if i == 0:
            full_b[0] = zero_layer
            full_b[1, pl.ds(0, rows), :] = -qz_b[1]
            full_b[1, pl.ds(rows, 8), :] = blank
            run(0, step - 1, 1, gather, 0)
            spread(-1, 0)
            grad_b[2 + layer(-2), pl.ds(0, rows), :] = full_b[1, pl.ds(0, rows), :]
            back_face.start()

            @pl.when(has_prev)
            def _():
                back_corner_prev.start()

            @pl.when(has_next)
            def _():
                back_corner_next.start()
        else:
            run(step * i - 1, step, 2, gather, 0)
            run(step * (i - 1), step, 2, spread, 0)
            send_back(i - 1)
    gather(slab - 1, 0)
    full_b[slab + 2, pl.ds(0, rows), :] = qz_b[slab]
    full_b[slab + 2, pl.ds(rows, 8), :] = blank
    run(slab - step, step, 2, spread, 0)
    send_back(CHUNKS - 1)

    row8 = lax.broadcasted_iota(jnp.int32, (8, cols), 0)

    def add(k, carry):
        z = layer(k)
        more = back_y[z]
        grad_b[2 + z, pl.ds(0, 8), :] = grad_b[2 + z, pl.ds(0, 8), :] + jnp.where(row8 < 2, more, 0.0)
        grad_b[2 + z, pl.ds(rows - 8, 8), :] = grad_b[2 + z, pl.ds(rows - 8, 8), :] + jnp.where(row8 > 5, more, 0.0)
        return carry

    outs = []
    for i in range(CHUNKS):
        start = chunk_start(i)
        if i == 0:
            back_face.wait_recv()

            @pl.when(has_prev)
            def _():
                back_corner_next.wait_recv()

            @pl.when(has_next)
            def _():
                back_corner_prev.wait_recv()

            near = 2 + layer(0)
            grad_b[near, pl.ds(0, rows), :] = grad_b[near, pl.ds(0, rows), :] + back_z[face_ext_in(core)]
            grad_b[near, pl.ds(0, 8), :] = grad_b[near, pl.ds(0, 8), :] + jnp.where(row8 < 1, back_d[0], 0.0)
            grad_b[near, pl.ds(rows - 8, 8), :] = grad_b[near, pl.ds(rows - 8, 8), :] + jnp.where(row8 > 6, back_d[0], 0.0)
            near = 2 + layer(1)
            grad_b[near, pl.ds(0, rows), :] = grad_b[near, pl.ds(0, rows), :] + back_z[1 - face_ext_in(core)]

        @pl.when(has_prev)
        def _(i=i):
            back_next(i).wait_recv()

        @pl.when(has_next)
        def _(i=i):
            back_prev(i).wait_recv()

        @pl.when(has_prev)
        def _(i=i):
            back_prev(i).wait_send()

        @pl.when(has_next)
        def _(i=i):
            back_next(i).wait_send()

        run(step * i, step, 2, add, 0)
        out = pltpu.make_async_copy(
            grad_b.at[pl.ds(2 + start, step), pl.ds(0, rows), :], grad_out.at[pl.ds(start, step)], out_sem.at[i]
        )
        out.start()
        outs.append(out)

    face.wait_send()
    back_face.wait_send()

    @pl.when(has_prev)
    def _():
        corner_prev.wait_send()
        back_corner_prev.wait_send()
        for i in range(CHUNKS):
            halo_prev(i).wait_send()

    @pl.when(has_next)
    def _():
        corner_next.wait_send()
        back_corner_next.wait_send()
        for i in range(CHUNKS):
            halo_next(i).wait_send()

    image_copy.wait()
    for out in outs:
        out.wait()


def face_ext(core, slab):
    return pl.ds(core * 1 + (1 - core) * (slab + 2), 1)


def face_ext_in(core):
    return 1 - core


def solution(mesh):
    tiles = mesh.shape["tile"]

    def shards(density, absorption, view_dir, target_ids, palette, coef, light):
        slab, rows, cols = density.shape
        ext = rows + 8
        f32 = jnp.float32
        kernel = functools.partial(body, tiles, slab, rows, cols, 2 * slab)
        scratch = [
            pltpu.VMEM((slab + 4, ext, cols), f32),
            pltpu.VMEM((slab + 2, ext, cols), f32),
            *[pltpu.VMEM((slab, rows, cols), f32)] * 5,
            pltpu.VMEM((slab + 1, rows, cols), f32),
            pltpu.VMEM((slab, ext, cols), f32),
            pltpu.VMEM((slab + 2, rows, cols), f32),
            pltpu.VMEM((slab + 3, ext, cols), f32),
            pltpu.VMEM((slab + 4, ext, cols), f32),
            pltpu.VMEM(absorption.shape, f32),
            pltpu.VMEM(target_ids.shape, jnp.int32),
            pltpu.VMEM(palette.shape, f32),
            pltpu.SMEM(view_dir.shape, jnp.int32),
            pltpu.SMEM(coef.shape, f32),
            pltpu.SMEM(light.shape, f32),
            pltpu.VMEM((3, rows, cols), f32),
            pltpu.VMEM((4, rows, cols), f32),
            pltpu.VMEM((4, rows, cols), f32),
            pltpu.VMEM((3, rows, cols), f32),
            pltpu.VMEM((slab, 8, cols), f32),
            pltpu.VMEM((2, rows, cols), f32),
            pltpu.VMEM((1, 8, cols), f32),
            pltpu.SemaphoreType.DMA,
            pltpu.SemaphoreType.DMA((6,)),
            pltpu.SemaphoreType.DMA((2, CHUNKS)),
            pltpu.SemaphoreType.DMA((2, CHUNKS)),
            pltpu.SemaphoreType.DMA((6,)),
            pltpu.SemaphoreType.DMA((6,)),
            pltpu.SemaphoreType.DMA,
            pltpu.SemaphoreType.DMA,
            pltpu.SemaphoreType.DMA((2, CHUNKS)),
            pltpu.SemaphoreType.DMA((2, CHUNKS)),
            pltpu.SemaphoreType.DMA((CHUNKS + 1,)),
        ]
        return pl.pallas_call(
            kernel,
            out_shape=(
                jax.ShapeDtypeStruct((3, rows // 2, cols), f32),
                jax.ShapeDtypeStruct(density.shape, f32),
            ),
            in_specs=[pl.BlockSpec(memory_space=pl.ANY)] * 7,
            out_specs=[pl.BlockSpec(memory_space=pl.ANY)] * 2,
            scratch_shapes=scratch,
            compiler_params=pltpu.CompilerParams(
                collective_id=0, has_side_effects=True, vmem_limit_bytes=24 * 1024 * 1024
            ),
            cost_estimate=pl.CostEstimate(flops=200 * slab * rows * cols, bytes_accessed=8 * slab * rows * cols, transcendentals=0),
        )(density, absorption, view_dir, target_ids, palette, coef, light)

    placed = (P("depth", "tile", None), P("tile", None), P("tile"), P("tile", None), P(), P(), P())
    return jax.shard_map(
        shards,
        mesh=mesh,
        in_specs=placed,
        out_specs=(P(None, ("tile", "depth"), None), P("depth", "tile", None)),
        check_vma=False,
    )
```

time: 82.9 us -> 32.9 us (0.40)
  the two profiles are of different devices: /device:TPU:254 before, /device:TPU:257 now
where the time goes in v1:
time: 32.9 us; the launch traced here: 32.6 us
  Pallas kernels  25.4 us (77%)
  local copies, waits for them, and re-layouts  6.54 us (20%)
  between operations  0.66 us (2%)
    pallas_call x1, Pallas kernels, shards(): pl.pallas_call(kernel, out_shape=(jax.ShapeDtypeStruct((3, rows // 2, col...  25.4 us
    unnamed x16, local copies, waits for them, and re-layouts  6.54 us

profile of v1, /device:TPU:257, one launch (start us, length us, event | category | flops | bytes accessed | tf_op | source)
XLA Modules:
  0.0 32.6 jit_solution(5354165095571336293)
XLA Ops:
  0.6 0.0 copy-start
  0.6 1.0 %copy-done = f32[32,16,256]{2,1,0:T(8,128)S(1)} copy-done((f32[32,16,256]{2,1,0:T(8,128)S(1)}, f32[32,16,256]{2,1,0:T(8,128)}, u32[]{:S(2)}) %copy-start) | copy-done | bytes 524312
  1.7 0.0 copy-start.1
  1.7 0.7 %copy-done.1 = f32[16,256]{1,0:T(8,128)S(1)} copy-done((f32[16,256]{1,0:T(8,128)S(1)}, f32[16,256]{1,0:T(8,128)}, u32[]{:S(2)}) %copy-start.1) | copy-done | bytes 16408
  2.4 0.0 copy-start.2
  2.4 0.7 %copy-done.2 = s32[16,256]{1,0:T(8,128)S(1)} copy-done((s32[16,256]{1,0:T(8,128)S(1)}, s32[16,256]{1,0:T(8,128)}, u32[]{:S(2)}) %copy-start.2) | copy-done | bytes 16408
  3.1 0.0 copy-start.3
  3.1 0.7 %copy-done.3 = f32[3,128]{1,0:T(4,128)S(1)} copy-done((f32[3,128]{1,0:T(4,128)S(1)}, f32[3,128]{1,0:T(4,128)}, u32[]{:S(2)}) %copy-start.3) | copy-done | bytes 1560
  3.8 0.0 copy-start.4
  3.8 0.7 %copy-done.4 = f32[3,4]{1,0:T(4,128)S(1)} copy-done((f32[3,4]{1,0:T(4,128)S(1)}, f32[3,4]{1,0:T(4,128)}, u32[]{:S(2)}) %copy-start.4) | copy-done | bytes 72
  4.5 0.0 copy-start.5
  4.5 0.7 %copy-done.5 = s32[16]{0:T(128)S(1)} copy-done((s32[16]{0:T(128)S(1)}, s32[16]{0:T(128)}, u32[]{:S(2)}) %copy-start.5) | copy-done | bytes 88
  5.1 0.0 copy-start.6
  5.1 0.7 %copy-done.6 = f32[3]{0:T(128)S(1)} copy-done((f32[3]{0:T(128)S(1)}, f32[3]{0:T(128)}, u32[]{:S(2)}) %copy-start.6) | copy-done | bytes 36
  5.8 25.4 %shard_map.86 = (f32[3,8,256]{2,1,0:T(8,128)S(1)}, f32[32,16,256]{2,1,0:T(8,128)S(1)}) custom-call(f32[32,16,256]{2,1,0:T(8,128)S(1)} %copy-done, f32[16,256]{1,0:T(8,128)S(1)} %copy-done.1, s32[16]{0:T(128)S(1)} %copy-done.5, s32[16,256]{1,0:T(8,128)S(1)} %copy-done.2, f32[3,128]{1,0:T(4,128)S(1)} %copy-done.3, f32[3,4]{1,0:T(4,128)S(1)} %copy-done.4, ...), custom_call_target="tpu_custom_call" | custom-call | flops 26214400 | bytes 1048576 | tf_op jit(solution)/shard_map/pallas_call | solution.py:537
  31.2 0.6 %copy.11 = f32[3,8,256]{2,1,0:T(8,128)} copy(f32[3,8,256]{2,1,0:T(8,128)S(1)} %get-tuple-element.4) | data formatting | bytes 49152
  31.8 0.8 %copy.12 = f32[32,16,256]{2,1,0:T(8,128)} copy(f32[32,16,256]{2,1,0:T(8,128)S(1)} %get-tuple-element.5) | data formatting | bytes 1048576
Async XLA Ops:
  0.6 1.0 %copy-start = (f32[32,16,256]{2,1,0:T(8,128)S(1)}, f32[32,16,256]{2,1,0:T(8,128)}, u32[]{:S(2)}) copy-start(f32[32,16,256]{2,1,0:T(8,128)} %density.1) | copy-start | bytes 1572868
  1.7 0.7 %copy-start.1 = (f32[16,256]{1,0:T(8,128)S(1)}, f32[16,256]{1,0:T(8,128)}, u32[]{:S(2)}) copy-start(f32[16,256]{1,0:T(8,128)} %absorption.1) | copy-start | bytes 49156
  2.4 0.7 %copy-start.2 = (s32[16,256]{1,0:T(8,128)S(1)}, s32[16,256]{1,0:T(8,128)}, u32[]{:S(2)}) copy-start(s32[16,256]{1,0:T(8,128)} %target_ids.1) | copy-start | bytes 49156
  3.1 0.7 %copy-start.3 = (f32[3,128]{1,0:T(4,128)S(1)}, f32[3,128]{1,0:T(4,128)}, u32[]{:S(2)}) copy-start(f32[3,128]{1,0:T(4,128)} %palette.1) | copy-start | bytes 4612
  3.8 0.7 %copy-start.4 = (f32[3,4]{1,0:T(4,128)S(1)}, f32[3,4]{1,0:T(4,128)}, u32[]{:S(2)}) copy-start(f32[3,4]{1,0:T(4,128)} %coef.1) | copy-start | bytes 148
  4.5 0.7 %copy-start.5 = (s32[16]{0:T(128)S(1)}, s32[16]{0:T(128)}, u32[]{:S(2)}) copy-start(s32[16]{0:T(128)} %view_dir.1) | copy-start | bytes 196
  5.1 0.7 %copy-start.6 = (f32[3]{0:T(128)S(1)}, f32[3]{0:T(128)}, u32[]{:S(2)}) copy-start(f32[3]{0:T(128)} %light.1) | copy-start | bytes 40

commit v2 on v1

--- a/solution.py
+++ b/solution.py
@@ -243,12 +243,12 @@
         def _(i=i):
             halo_prev(i).wait_recv()
 
-        run(step * i - 1, step, 2, blur_one, 0)
+        run(step * i - 1, step, 8, blur_one, 0)
         if i:
-            depth = run(step * (i - 1), step, 2, shade, depth)
+            depth = run(step * (i - 1), step, 8, shade, depth)
     blur(slab - 1)
     smooth[slab + 1] = field[2 + layer(slab - 1)]
-    depth = run(slab - step, step, 2, shade, depth)
+    depth = run(slab - step, step, 8, shade, depth)
 
     toward = jnp.where(ascending, -1.0, 1.0)
     base = jnp.where(ascending, 0.0, -depth)
@@ -271,7 +271,7 @@
     edge_b[slab] = depth
     zero = jnp.zeros((rows, cols), jnp.float32)
     left = lax.exp2(base)
-    right, m0, m1, m2, m3 = run(0, slab, 2, composite, (left, zero, zero, zero, zero))
+    right, m0, m1, m2, m3 = run(0, slab, 8, composite, (left, zero, zero, zero, zero))
     edge_b[slab] = right
     for c in range(3):
         mine[c] = coef_s[c, 0] * m0 + (coef_s[c, 1] / 8.0) * m1 + (coef_s[c, 2] / 64.0) * m2 + (coef_s[c, 3] / 512.0) * m3
@@ -382,7 +382,7 @@
     qz_b[0] = zero
     qz_b[slab + 1] = zero
     for i in range(CHUNKS):
-        rest = run(step * i, step, 2, pull, rest)
+        rest = run(step * i, step, 8, pull, rest)
         if i == 0:
             full_b[0] = zero_layer
             full_b[1, pl.ds(0, rows), :] = -qz_b[1]
@@ -400,13 +400,13 @@
             def _():
                 back_corner_next.start()
         else:
-            run(step * i - 1, step, 2, gather, 0)
-            run(step * (i - 1), step, 2, spread, 0)
+            run(step * i - 1, step, 8, gather, 0)
+            run(step * (i - 1), step, 8, spread, 0)
             send_back(i - 1)
     gather(slab - 1, 0)
     full_b[slab + 2, pl.ds(0, rows), :] = qz_b[slab]
     full_b[slab + 2, pl.ds(rows, 8), :] = blank
-    run(slab - step, step, 2, spread, 0)
+    run(slab - step, step, 8, spread, 0)
     send_back(CHUNKS - 1)
 
     row8 = lax.broadcasted_iota(jnp.int32, (8, cols), 0)
@@ -455,7 +455,7 @@
         def _(i=i):
             back_next(i).wait_send()
 
-        run(step * i, step, 2, add, 0)
+        run(step * i, step, 8, add, 0)
         out = pltpu.make_async_copy(
             grad_b.at[pl.ds(2 + start, step), pl.ds(0, rows), :], grad_out.at[pl.ds(start, step)], out_sem.at[i]
         )
@@ -547,7 +547,7 @@
                 collective_id=0, has_side_effects=True, vmem_limit_bytes=24 * 1024 * 1024
             ),
             cost_estimate=pl.CostEstimate(flops=200 * slab * rows * cols, bytes_accessed=8 * slab * rows * cols, transcendentals=0),
-        )(density, absorption, view_dir, target_ids, palette, coef, light)
+        )(*[pltpu.with_memory_space_constraint(x, pltpu.HBM) for x in (density, absorption, view_dir, target_ids, palette, coef, light)])
 
     placed = (P("depth", "tile", None), P("tile", None), P("tile"), P("tile", None), P(), P(), P())
     return jax.shard_map(

time: 32.9 us -> 23.9 us (0.73)
  local copies, waits for them, and re-layouts: 6.54 us -> 1.4 us
  Pallas kernels: 25.4 us -> 21.7 us
    unnamed x16 -> x2, local copies, waits for them, and re-layouts: 6.54 us -> 1.4 us
    pallas_call x1, Pallas kernels: 25.4 us -> 21.7 us  [shards(): pl.pallas_call(kernel, out_shape=(jax.ShapeDtypeStruct((3, rows // 2, col...]
where the time goes in v2:
time: 23.9 us; the launch traced here: 23.7 us
  Pallas kernels  21.7 us (91%)
  local copies, waits for them, and re-layouts  1.4 us (6%)
  between operations  0.64 us (3%)
    pallas_call x1, Pallas kernels, shards(): pl.pallas_call(kernel, out_shape=(jax.ShapeDtypeStruct((3, rows // 2, col...  21.7 us
    unnamed x2, local copies, waits for them, and re-layouts  1.4 us

profile of v2, /device:TPU:257, one launch (start us, length us, event | category | flops | bytes accessed | tf_op | source)
XLA Modules:
  0.0 23.7 jit_solution(8840852115859863653)
XLA Ops:
  0.6 21.7 %shard_map.86 = (f32[3,8,256]{2,1,0:T(8,128)S(1)}, f32[32,16,256]{2,1,0:T(8,128)S(1)}) custom-call(f32[32,16,256]{2,1,0:T(8,128)} %density.1, f32[16,256]{1,0:T(8,128)} %absorption.1, s32[16]{0:T(128)} %view_dir.1, s32[16,256]{1,0:T(8,128)} %target_ids.1, f32[3,128]{1,0:T(4,128)} %palette.1, f32[3,4]{1,0:T(4,128)} %coef.1, f32[3]{0:T(128)} %light.1), custom_call_target="tpu_custom_call" | custom-call | flops 26214400 | bytes 1048576 | tf_op jit(solution)/shard_map/pallas_call | solution.py:537
  22.3 0.6 %copy.11 = f32[3,8,256]{2,1,0:T(8,128)} copy(f32[3,8,256]{2,1,0:T(8,128)S(1)} %get-tuple-element.4) | data formatting | bytes 49152
  22.9 0.8 %copy.12 = f32[32,16,256]{2,1,0:T(8,128)} copy(f32[32,16,256]{2,1,0:T(8,128)S(1)} %get-tuple-element.5) | data formatting | bytes 1048576

commit v3 on v2

v3 whole, which is shorter than its diff:
```python
import functools
import math

import jax
import jax.numpy as jnp
from jax import lax
from jax.experimental import pallas as pl
from jax.experimental.pallas import tpu as pltpu
from jax.sharding import PartitionSpec as P

MESH = pl.DeviceIdType.MESH
LOG2E = math.log2(math.e)
CHUNKS = 4


def body(
    tiles, slab, rows, cols, depth_count,
    density, absorption, view_dir, target_ids, palette, coef, light,
    image_v, grad_b, back_y,
    field, smooth, shade_b, cz_b, cy_b, cx_b, fac_b, edge_b, ay_b, qz_b, full_b,
    ab_v, ids_v, pal_v, view_s, coef_s, light_s, mine, theirs, tgt_v, back_z, colours,
    load_sem, small_sem, halo_send, halo_recv, core_send, core_recv, ret_send, ret_recv,
):
    tile = lax.axis_index("tile")
    core = lax.axis_index("depth")
    other = 1 - core
    has_prev = tile > 0
    has_next = tile < tiles - 1
    ext = rows + 8
    step = slab // CHUNKS
    sign = 2 * core - 1
    first = (1 - core) * (slab - 1)

    def layer(k):
        return first + sign * k

    def chunk_start(i):
        return core * (step * i) + other * (slab - step - step * i)

    prev_id = (jnp.maximum(tile - 1, 0), core)
    next_id = (jnp.minimum(tile + 1, tiles - 1), core)
    across_id = (tile, other)

    def rx(value, shift):
        return pltpu.roll(value, shift % cols, 1)

    def ry(value, shift):
        return pltpu.roll(value, shift % ext, 0)

    barrier = pltpu.get_barrier_semaphore()
    pl.semaphore_signal(barrier, inc=1, device_id=across_id, device_id_type=MESH)

    @pl.when(has_prev)
    def _():
        pl.semaphore_signal(barrier, inc=1, device_id=prev_id, device_id_type=MESH)

    @pl.when(has_next)
    def _():
        pl.semaphore_signal(barrier, inc=1, device_id=next_id, device_id_type=MESH)

    own = pltpu.make_async_copy(density, field.at[pl.ds(2, slab), pl.ds(0, rows), :], load_sem)
    own.start()
    smalls = [
        pltpu.make_async_copy(src, dst, small_sem.at[n])
        for n, (src, dst) in enumerate(
            [(view_dir, view_s), (absorption, ab_v), (light, light_s), (coef, coef_s), (target_ids, ids_v), (palette, pal_v)]
        )
    ]
    for copy in smalls:
        copy.start()

    zero_layer = jnp.zeros((ext, cols), jnp.float32)
    field[2 + layer(slab)] = zero_layer

    def clear_rows(at_field, at_back):
        def clear(j, carry):
            field[2 + j, pl.ds(at_field, 2), :] = jnp.zeros((2, cols), jnp.float32)
            back_y[j, pl.ds(at_back, 2), :] = jnp.zeros((2, cols), jnp.float32)
            return carry

        lax.fori_loop(0, slab, clear, 0)

    @pl.when(jnp.logical_not(has_prev))
    def _():
        clear_rows(rows + 6, 0)

    @pl.when(jnp.logical_not(has_next))
    def _():
        clear_rows(rows, 6)

    pl.semaphore_wait(barrier, 1 + has_prev.astype(jnp.int32) + has_next.astype(jnp.int32))

    def across(src, dst, n):
        return pltpu.make_async_remote_copy(
            src, dst, core_send.at[n], core_recv.at[n], device_id=across_id, device_id_type=MESH
        )

    face = across(
        density.at[pl.ds(other * (slab - 2), 2)], field.at[pl.ds(core * (slab + 2), 2), pl.ds(0, rows), :], 0
    )
    corner = across(
        field.at[pl.ds(2 + other * (slab - 1), 1), pl.ds(rows, 8), :],
        field.at[pl.ds(2 + core * slab - other, 1), pl.ds(rows, 8), :],
        1,
    )

    def halo_prev(i):
        start = chunk_start(i)
        return pltpu.make_async_remote_copy(
            density.at[pl.ds(start, step), pl.ds(0, 2), :],
            field.at[pl.ds(2 + start, step), pl.ds(rows, 2), :],
            halo_send.at[0, i], halo_recv.at[0, i], device_id=prev_id, device_id_type=MESH,
        )

    def halo_next(i):
        start = chunk_start(i)
        return pltpu.make_async_remote_copy(
            density.at[pl.ds(start, step), pl.ds(rows - 2, 2), :],
            field.at[pl.ds(2 + start, step), pl.ds(rows + 6, 2), :],
            halo_send.at[1, i], halo_recv.at[1, i], device_id=next_id, device_id_type=MESH,
        )

    for i in range(CHUNKS):

        @pl.when(has_prev)
        def _(i=i):
            halo_prev(i).start()

        @pl.when(has_next)
        def _(i=i):
            halo_next(i).start()

        if i == 0:
            face.start()

    def halo_arrived(i):
        @pl.when(has_prev)
        def _():
            halo_next(i).wait_recv()

        @pl.when(has_next)
        def _():
            halo_prev(i).wait_recv()

    for copy in smalls:
        copy.wait()
    row_of = lax.broadcasted_iota(jnp.int32, (rows, cols), 0)
    view = jnp.zeros((rows, cols), jnp.int32)
    for y in range(rows):
        view = jnp.where(row_of == y, view_s[y], view)
    ascending = view == other
    absorb = ab_v[...]
    half_light = [0.5 * light_s[0] * sign.astype(jnp.float32), 0.5 * light_s[1], 0.5 * light_s[2]]
    for c in range(3):
        table = jnp.broadcast_to(pal_v[pl.ds(c, 1), :], (8, pal_v.shape[1]))
        for y in range(0, rows, 8):
            for x in range(0, cols, 128):
                picked = jnp.take_along_axis(table, ids_v[pl.ds(y, 8), pl.ds(x, 128)], axis=1, mode="promise_in_bounds")
                tgt_v[c, pl.ds(y, 8), pl.ds(x, 128)] = picked

    own.wait()
    face.wait_recv()
    halo_arrived(0)
    corner.start()

    def blur(k):
        at = 2 + layer(k)
        here = field[at]
        total = 2.0 * here + field[at - 1] + field[at + 1]
        total = total + (ry(here, 1) + ry(here, -1)) + (rx(here, 1) + rx(here, -1))
        smooth[k + 1] = total

    scale = absorb * (LOG2E / depth_count)
    slope = absorb * (1.0 / (8.0 * depth_count))

    def shade(k, depth):
        here = smooth[k + 1]
        mid = here[:rows]
        dz = smooth[k + 2, pl.ds(0, rows), :] - smooth[k, pl.ds(0, rows), :]
        dy = ry(here, -1)[:rows] - ry(here, 1)[:rows]
        dx = rx(mid, -1) - rx(mid, 1)
        inv = lax.rsqrt(256.0 + dz * dz + dy * dy + dx * dx)
        facing = (half_light[0] * dz + half_light[1] * dy + half_light[2] * dx) * inv
        bend = facing * inv
        shade_b[k] = 0.5 + facing
        cz_b[k] = inv * (half_light[0] - bend * dz)
        cy_b[k] = inv * (half_light[1] - bend * dy)
        cx_b[k] = inv * (half_light[2] - bend * dx)
        power = mid * (LOG2E / 8.0)
        plus = jnp.log(1.0 + lax.exp2(power))
        fac_b[k] = slope * lax.exp2(power - plus * LOG2E)
        edge_b[k] = depth
        return depth + scale * plus

    def run(lo, count, unroll, one, carry):
        def several(j, carry):
            for u in range(unroll):
                carry = one(lo + j * unroll + u, carry)
            return carry

        return lax.fori_loop(0, count // unroll, several, carry)

    def blur_one(k, carry):
        blur(k)
        return carry

    zero = jnp.zeros((rows, cols), jnp.float32)
    tail = zero
    halo_arrived(1)
    run(1, 2 * step - 2, step - 1, blur_one, 0)
    tail = run(2, 2 * step - 4, step - 2, shade, tail)
    for i in range(2, CHUNKS - 1):
        halo_arrived(i)
        run(step * i - 1, step, step, blur_one, 0)
        tail = run(step * i - 2, step, step, shade, tail)
    halo_arrived(CHUNKS - 1)
    run(slab - step - 1, step + 1, step + 1, blur_one, 0)
    smooth[slab + 1] = field[2 + layer(slab - 1)]
    tail = run(slab - step - 2, step + 2, step + 2, shade, tail)
    corner.wait_recv()
    run(-1, 2, 2, blur_one, 0)
    depth0 = shade(0, zero)
    depth1 = shade(1, depth0)
    edge_b[0] = -depth1
    edge_b[1] = depth0 - depth1
    edge_b[slab] = tail
    depth = tail + depth1

    toward = jnp.where(ascending, -1.0, 1.0)
    base = jnp.where(ascending, -depth1, depth1 - depth)

    def composite(k, carry):
        left, m0, m1, m2, m3 = carry
        right = lax.exp2(toward * edge_b[k + 1] + base)
        mid = smooth[k + 1, pl.ds(0, rows), :]
        part = jnp.abs(left - right) * shade_b[k]
        m0 = m0 + part
        part = part * mid
        m1 = m1 + part
        part = part * mid
        m2 = m2 + part
        part = part * mid
        m3 = m3 + part
        edge_b[k] = left
        return (right, m0, m1, m2, m3)

    left = lax.exp2(base - toward * depth1)
    right, m0, m1, m2, m3 = run(0, slab, 8, composite, (left, zero, zero, zero, zero))
    edge_b[slab] = right
    for c in range(3):
        mine[c] = coef_s[c, 0] * m0 + (coef_s[c, 1] / 8.0) * m1 + (coef_s[c, 2] / 64.0) * m2 + (coef_s[c, 3] / 512.0) * m3
    mine[3] = depth
    swap = across(mine, theirs, 2)
    swap.start()
    swap.wait_recv()

    enter = jnp.where(ascending, lax.exp2(-theirs[3]), 1.0)
    leave = lax.exp2(-depth)
    misfit = []
    before = jnp.zeros((rows, cols), jnp.float32)
    for c in range(3):
        colour = jnp.where(ascending, theirs[c] + enter * mine[c], mine[c] + leave * theirs[c])
        colours[c] = colour
        gap = (colour - tgt_v[c]) * float(depth_count)
        misfit.append(gap)
        before = before + gap * jnp.where(ascending, mine[c], theirs[c])
    rest = jnp.where(ascending, enter, leave) * before
    share = rows // 2
    mine_rows = pl.ds(pl.multiple_of(core * share, 8), share)
    for c in range(3):
        image_v[c] = colours[c, mine_rows, :]
    ramp = [
        enter
        * (misfit[0] * coef_s[0, i] + misfit[1] * coef_s[1, i] + misfit[2] * coef_s[2, i])
        * (1.0 / 8.0**i)
        for i in range(4)
    ]
    ramp2 = 2.0 * ramp[2]
    ramp3 = 3.0 * ramp[3]
    blank = jnp.zeros((8, cols), jnp.float32)

    def pull(k, rest):
        left = edge_b[k]
        signed = left - edge_b[k + 1]
        weight = jnp.abs(signed)
        mid = smooth[k + 1, pl.ds(0, rows), :]
        lit = shade_b[k]
        value = ramp[0] + mid * (ramp[1] + mid * (ramp[2] + mid * ramp[3]))
        deriv = ramp[1] + mid * (ramp2 + mid * ramp3)
        shown = lit * value
        pulled = weight * value
        direct = weight * lit * deriv + (left * shown - rest) * fac_b[k]
        qx = pulled * cx_b[k]
        qy = jnp.concatenate([pulled * cy_b[k], blank], 0)
        direct = direct + rx(qx, 1) - rx(qx, -1)
        ay_b[k] = ry(qy, 1) - ry(qy, -1) + jnp.concatenate([direct, blank], 0)
        qz_b[k + 1] = pulled * cz_b[k]
        return rest - signed * shown

    def gather(k, carry):
        full_b[k + 2, pl.ds(0, rows), :] = ay_b[k, pl.ds(0, rows), :] + qz_b[k] - qz_b[k + 2]
        full_b[k + 2, pl.ds(rows, 8), :] = ay_b[k, pl.ds(rows, 8), :]
        return carry

    def spread(k, carry):
        here = full_b[k + 2]
        total = 2.0 * here + full_b[k + 1] + full_b[k + 3]
        total = total + (ry(here, 1) + ry(here, -1)) + (rx(here, 1) + rx(here, -1))
        grad_b[2 + layer(k)] = total
        return carry

    def back_prev(i):
        start = chunk_start(i)
        return pltpu.make_async_remote_copy(
            grad_b.at[pl.ds(2 + start, step), pl.ds(rows + 6, 2), :],
            back_y.at[pl.ds(start, step), pl.ds(6, 2), :],
            ret_send.at[0, i], ret_recv.at[0, i], device_id=prev_id, device_id_type=MESH,
        )

    def back_next(i):
        start = chunk_start(i)
        return pltpu.make_async_remote_copy(
            grad_b.at[pl.ds(2 + start, step), pl.ds(rows, 2), :],
            back_y.at[pl.ds(start, step), pl.ds(0, 2), :],
            ret_send.at[1, i], ret_recv.at[1, i], device_id=next_id, device_id_type=MESH,
        )

    back_face = across(grad_b.at[pl.ds(other * (slab + 2), 2)], back_z, 3)

    def send_back(i):
        @pl.when(has_prev)
        def _():
            back_prev(i).start()

        @pl.when(has_next)
        def _():
            back_next(i).start()

    qz_b[0] = zero
    qz_b[slab + 1] = zero
    rest = run(0, 2, 2, pull, rest)
    full_b[0] = zero_layer
    full_b[1, pl.ds(0, rows), :] = -qz_b[1]
    full_b[1, pl.ds(rows, 8), :] = blank
    gather(0, 0)
    spread(-1, 0)
    grad_b[2 + layer(-2)] = full_b[1]
    back_face.start()
    for i in range(CHUNKS - 1):
        rest = run(step * i + 2, step, step, pull, rest)
        run(step * i + 1, step, step, gather, 0)
        run(step * i, step, step, spread, 0)
        if i:
            send_back(i)
    run(slab - step + 2, step - 2, step - 2, pull, rest)
    run(slab - step + 1, step - 1, step - 1, gather, 0)
    full_b[slab + 2, pl.ds(0, rows), :] = qz_b[slab]
    full_b[slab + 2, pl.ds(rows, 8), :] = blank
    run(slab - step, step, step, spread, 0)
    send_back(CHUNKS - 1)

    back_face.wait_recv()
    near = 2 + layer(0)
    grad_b[near] = grad_b[near] + back_z[other]
    near = 2 + layer(1)
    grad_b[near] = grad_b[near] + back_z[core]
    send_back(0)

    face.wait_send()
    corner.wait_send()
    swap.wait_send()
    back_face.wait_send()

    @pl.when(has_prev)
    def _():
        for i in range(CHUNKS):
            halo_prev(i).wait_send()

    @pl.when(has_next)
    def _():
        for i in range(CHUNKS):
            halo_next(i).wait_send()

    for i in (*range(1, CHUNKS), 0):

        @pl.when(has_prev)
        def _(i=i):
            back_prev(i).wait_send()
            back_next(i).wait_recv()

        @pl.when(has_next)
        def _(i=i):
            back_next(i).wait_send()
            back_prev(i).wait_recv()


def finish(image_v, grad_b, back_y, image_out, grad_out, total, sems):
    slab, rows, cols = total.shape
    step = slab // CHUNKS
    image_copy = pltpu.make_async_copy(image_v, image_out, sems.at[CHUNKS])
    image_copy.start()
    row8 = lax.broadcasted_iota(jnp.int32, (8, cols), 0)
    outs = []
    for i in range(CHUNKS):
        for z in range(step * i, step * i + step):
            more = back_y[z]
            total[z, pl.ds(0, 8), :] = grad_b[2 + z, pl.ds(0, 8), :] + jnp.where(row8 < 2, more, 0.0)
            total[z, pl.ds(rows - 8, 8), :] = grad_b[2 + z, pl.ds(rows - 8, 8), :] + jnp.where(row8 > 5, more, 0.0)
        out = pltpu.make_async_copy(total.at[pl.ds(step * i, step)], grad_out.at[pl.ds(step * i, step)], sems.at[i])
        out.start()
        outs.append(out)
    image_copy.wait()
    for out in outs:
        out.wait()


def solution(mesh):
    tiles = mesh.shape["tile"]

    def shards(density, absorption, view_dir, target_ids, palette, coef, light):
        slab, rows, cols = density.shape
        ext = rows + 8
        f32 = jnp.float32
        kernel = functools.partial(body, tiles, slab, rows, cols, 2 * slab)
        scratch = [
            pltpu.VMEM((slab + 4, ext, cols), f32),
            pltpu.VMEM((slab + 2, ext, cols), f32),
            *[pltpu.VMEM((slab, rows, cols), f32)] * 5,
            pltpu.VMEM((slab + 1, rows, cols), f32),
            pltpu.VMEM((slab, ext, cols), f32),
            pltpu.VMEM((slab + 2, rows, cols), f32),
            pltpu.VMEM((slab + 3, ext, cols), f32),
            pltpu.VMEM(absorption.shape, f32),
            pltpu.VMEM(target_ids.shape, jnp.int32),
            pltpu.VMEM(palette.shape, f32),
            pltpu.SMEM(view_dir.shape, jnp.int32),
            pltpu.SMEM(coef.shape, f32),
            pltpu.SMEM(light.shape, f32),
            pltpu.VMEM((4, rows, cols), f32),
            pltpu.VMEM((4, rows, cols), f32),
            pltpu.VMEM((3, rows, cols), f32),
            pltpu.VMEM((2, ext, cols), f32),
            pltpu.VMEM((3, rows, cols), f32),
            pltpu.SemaphoreType.DMA,
            pltpu.SemaphoreType.DMA((6,)),
            pltpu.SemaphoreType.DMA((2, CHUNKS)),
            pltpu.SemaphoreType.DMA((2, CHUNKS)),
            pltpu.SemaphoreType.DMA((4,)),
            pltpu.SemaphoreType.DMA((4,)),
            pltpu.SemaphoreType.DMA((2, CHUNKS)),
            pltpu.SemaphoreType.DMA((2, CHUNKS)),
        ]
        image, grad, back = pl.pallas_call(
            kernel,
            out_shape=(
                pltpu.VMEM((3, rows // 2, cols), f32),
                pltpu.VMEM((slab + 4, ext, cols), f32),
                pltpu.VMEM((slab, 8, cols), f32),
            ),
            in_specs=[pl.BlockSpec(memory_space=pl.ANY)] * 7,
            out_specs=[pl.BlockSpec(memory_space=pltpu.VMEM)] * 3,
            scratch_shapes=scratch,
            compiler_params=pltpu.CompilerParams(
                collective_id=0, has_side_effects=True, vmem_limit_bytes=24 * 1024 * 1024
            ),
            cost_estimate=pl.CostEstimate(flops=200 * slab * rows * cols, bytes_accessed=8 * slab * rows * cols, transcendentals=0),
        )(*[pltpu.with_memory_space_constraint(x, pltpu.HBM) for x in (density, absorption, view_dir, target_ids, palette, coef, light)])
        return pl.pallas_call(
            finish,
            out_shape=(jax.ShapeDtypeStruct(image.shape, f32), jax.ShapeDtypeStruct(density.shape, f32)),
            in_specs=[pl.BlockSpec(memory_space=pltpu.VMEM)] * 3,
            out_specs=[pl.BlockSpec(memory_space=pl.ANY)] * 2,
            scratch_shapes=[pltpu.VMEM(density.shape, f32), pltpu.SemaphoreType.DMA((CHUNKS + 1,))],
            compiler_params=pltpu.CompilerParams(vmem_limit_bytes=8 * 1024 * 1024),
        )(image, grad, back)

    placed = (P("depth", "tile", None), P("tile", None), P("tile"), P("tile", None), P(), P(), P())
    return jax.shard_map(
        shards,
        mesh=mesh,
        in_specs=placed,
        out_specs=(P(None, ("tile", "depth"), None), P("depth", "tile", None)),
        check_vma=False,
    )
```

time: 23.9 us -> 23.2 us (0.971)
  local copies, waits for them, and re-layouts: 1.4 us -> 0 us
  Pallas kernels: 21.7 us -> 22.5 us
    unnamed x2 -> x0, local copies, waits for them, and re-layouts: 1.4 us -> none
    pallas_call x1 -> x2, Pallas kernels: 21.7 us -> 22.5 us  [the longest x1 21.6 us: shards(): pl.pallas_call(kernel, out_shape=(pltpu.VMEM((3, rows // 2, cols), f32),...]
where the time goes in v3:
time: 23.2 us; the launch traced here: 23.1 us
  Pallas kernels  22.5 us (97%)
  between operations  0.64 us (3%)
    pallas_call x1, Pallas kernels, shards(): pl.pallas_call(kernel, out_shape=(pltpu.VMEM((3, rows // 2, cols), f32),...  21.6 us
    pallas_call x1, Pallas kernels, shards(): pl.pallas_call(finish, out_shape=(jax.ShapeDtypeStruct(image.shape, f32),...  0.84 us

profile of v3, /device:TPU:257, one launch (start us, length us, event | category | flops | bytes accessed | tf_op | source)
XLA Modules:
  0.0 23.1 jit_solution(10230214502628641892)
XLA Ops:
  0.6 21.6 %shard_map.86 = (f32[3,8,256]{2,1,0:T(8,128)S(1)}, f32[36,24,256]{2,1,0:T(8,128)S(1)}, f32[32,8,256]{2,1,0:T(8,128)S(1)}) custom-call(f32[32,16,256]{2,1,0:T(8,128)} %density.1, f32[16,256]{1,0:T(8,128)} %absorption.1, s32[16]{0:T(128)} %view_dir.1, s32[16,256]{1,0:T(8,128)} %target_ids.1, f32[3,128]{1,0:T(4,128)} %palette.1, f32[3,4]{1,0:T(4,128)} %coef.1, ...), custom_call_target="tpu_custom_call" | custom-call | flops 26214400 | bytes 1048576 | tf_op jit(solution)/shard_map/pallas_call | solution.py:453
  22.3 0.8 %shard_map.87 = (f32[3,8,256]{2,1,0:T(8,128)}, f32[32,16,256]{2,1,0:T(8,128)}) custom-call(f32[3,8,256]{2,1,0:T(8,128)S(1)} %get-tuple-element.5.image_v, f32[36,24,256]{2,1,0:T(8,128)S(1)} %get-tuple-element.6.grad_b, f32[32,8,256]{2,1,0:T(8,128)S(1)} %get-tuple-element.7.back_y), custom_call_target="tpu_custom_call" | custom-call | tf_op jit(solution)/shard_map/pallas_call | solution.py:468

commit v4 on v3

v4 whole, which is shorter than its diff:
```python
import functools
import math

import jax
import jax.numpy as jnp
from jax import lax
from jax.experimental import pallas as pl
from jax.experimental.pallas import tpu as pltpu
from jax.sharding import PartitionSpec as P

MESH = pl.DeviceIdType.MESH
LOG2E = math.log2(math.e)
CHUNKS = 4
HALO = 4


def run(lo, count, unroll, one, carry):
    def several(j, carry):
        for u in range(unroll):
            carry = one(lo + j * unroll + u, carry)
        return carry

    return lax.fori_loop(0, count // unroll, several, carry)


def forward(
    tiles, slab, rows, cols, depth_count,
    density, absorption, view_dir, target_ids, palette, coef, light,
    smooth, shade_b, cz_b, cy_b, cx_b, fac_b, edge_b, ramp_b, image_v,
    field, info, plus_b, inv_b, ids_v, pal_v, view_s, coef_s, light_s, mine, theirs, colours,
    load_sem, small_sem, halo_send, halo_recv, core_send, core_recv,
):
    tile = lax.axis_index("tile")
    core = lax.axis_index("depth")
    other = 1 - core
    has_prev = tile > 0
    has_next = tile < tiles - 1
    ext = rows + 2 * HALO
    step = slab // CHUNKS
    sign = 2 * core - 1
    first = (1 - core) * (slab - 1)

    def layer(k):
        return first + sign * k

    def chunk_start(i):
        return core * (step * i) + other * (slab - step - step * i)

    prev_id = (jnp.maximum(tile - 1, 0), core)
    next_id = (jnp.minimum(tile + 1, tiles - 1), core)
    across_id = (tile, other)

    def rx(value, shift):
        return pltpu.roll(value, shift % cols, 1)

    def ry(value, shift):
        return pltpu.roll(value, shift % ext, 0)

    barrier = pltpu.get_barrier_semaphore()
    pl.semaphore_signal(barrier, inc=1, device_id=across_id, device_id_type=MESH)

    @pl.when(has_prev)
    def _():
        pl.semaphore_signal(barrier, inc=1, device_id=prev_id, device_id_type=MESH)

    @pl.when(has_next)
    def _():
        pl.semaphore_signal(barrier, inc=1, device_id=next_id, device_id_type=MESH)

    own = pltpu.make_async_copy(density, field.at[pl.ds(HALO, slab), pl.ds(0, rows), :], load_sem)
    smalls = [
        pltpu.make_async_copy(src, dst, small_sem.at[n])
        for n, (src, dst) in enumerate(
            [
                (view_dir, view_s),
                (absorption, info.at[0, pl.ds(0, rows), :]),
                (light, light_s),
                (coef, coef_s),
                (target_ids, ids_v),
                (palette, pal_v),
            ]
        )
    ]
    for copy in smalls:
        copy.start()
    own.start()

    field[HALO + layer(slab)] = jnp.zeros((ext, cols), jnp.float32)

    def clear_rows(at):
        def clear(j, carry):
            field[HALO + j, pl.ds(at, HALO), :] = jnp.zeros((HALO, cols), jnp.float32)
            return carry

        lax.fori_loop(0, slab, clear, 0)
        for n in range(5):
            info[n, pl.ds(at, HALO), :] = jnp.zeros((HALO, cols), jnp.float32)

    @pl.when(jnp.logical_not(has_prev))
    def _():
        clear_rows(rows + HALO)

    @pl.when(jnp.logical_not(has_next))
    def _():
        clear_rows(rows)

    pl.semaphore_wait(barrier, 1 + has_prev.astype(jnp.int32) + has_next.astype(jnp.int32))

    def across(src, dst, n):
        return pltpu.make_async_remote_copy(
            src, dst, core_send.at[n], core_recv.at[n], device_id=across_id, device_id_type=MESH
        )

    face_at = core * (slab + HALO)
    face = across(
        density.at[pl.ds(other * (slab - HALO), HALO)], field.at[pl.ds(face_at, HALO), pl.ds(0, rows), :], 0
    )
    corner = across(
        field.at[pl.ds(HALO + other * (slab - HALO), HALO), pl.ds(rows, 2 * HALO), :],
        field.at[pl.ds(face_at, HALO), pl.ds(rows, 2 * HALO), :],
        1,
    )

    def to_prev(src, dst, n):
        return pltpu.make_async_remote_copy(
            src, dst, halo_send.at[0, n], halo_recv.at[0, n], device_id=prev_id, device_id_type=MESH
        )

    def to_next(src, dst, n):
        return pltpu.make_async_remote_copy(
            src, dst, halo_send.at[1, n], halo_recv.at[1, n], device_id=next_id, device_id_type=MESH
        )

    low, high = pl.ds(0, HALO), pl.ds(rows - HALO, HALO)
    after, before_rows = pl.ds(rows, HALO), pl.ds(rows + HALO, HALO)

    def halo_prev(i):
        if i == CHUNKS:
            return to_prev(info.at[:, low, :], info.at[:, after, :], i)
        start = chunk_start(i)
        return to_prev(density.at[pl.ds(start, step), low, :], field.at[pl.ds(HALO + start, step), after, :], i)

    def halo_next(i):
        if i == CHUNKS:
            return to_next(info.at[:, high, :], info.at[:, before_rows, :], i)
        start = chunk_start(i)
        return to_next(density.at[pl.ds(start, step), high, :], field.at[pl.ds(HALO + start, step), before_rows, :], i)

    def halo_start(i):
        @pl.when(has_prev)
        def _():
            halo_prev(i).start()

        @pl.when(has_next)
        def _():
            halo_next(i).start()

    def halo_arrived(i):
        @pl.when(has_prev)
        def _():
            halo_next(i).wait_recv()

        @pl.when(has_next)
        def _():
            halo_prev(i).wait_recv()

    halo_start(0)
    face.start()
    for i in range(1, CHUNKS):
        halo_start(i)

    for copy in smalls:
        copy.wait()
    own_row = lax.broadcasted_iota(jnp.int32, (rows, cols), 0)
    view = jnp.zeros((rows, cols), jnp.int32)
    for y in range(rows):
        view = jnp.where(own_row == y, view_s[y], view)
    info[1, pl.ds(0, rows), :] = view.astype(jnp.float32)
    for c in range(3):
        table = jnp.broadcast_to(pal_v[pl.ds(c, 1), :], (8, pal_v.shape[1]))
        for y in range(0, rows, 8):
            for x in range(0, cols, 128):
                picked = jnp.take_along_axis(table, ids_v[pl.ds(y, 8), pl.ds(x, 128)], axis=1, mode="promise_in_bounds")
                info[2 + c, pl.ds(y, 8), pl.ds(x, 128)] = picked
    halo_start(CHUNKS)
    half_light = [0.5 * light_s[0] * sign.astype(jnp.float32), 0.5 * light_s[1], 0.5 * light_s[2]]

    own.wait()
    halo_arrived(0)
    corner.start()
    halo_arrived(CHUNKS)
    absorb = info[0]
    ascending = info[1] == other.astype(jnp.float32)
    scale = absorb * (LOG2E / depth_count)
    slope = absorb * (1.0 / (8.0 * depth_count))

    def blur(k, carry):
        at = HALO + layer(k)
        here = field[at]
        total = 2.0 * here + field[at - 1] + field[at + 1]
        total = total + (ry(here, 1) + ry(here, -1)) + (rx(here, 1) + rx(here, -1))
        smooth[k + 3] = total
        return carry

    def shade(k):
        here = smooth[k + 3]
        dz = smooth[k + 4] - smooth[k + 2]
        dy = ry(here, -1) - ry(here, 1)
        dx = rx(here, -1) - rx(here, 1)
        inv = lax.rsqrt(256.0 + dz * dz + dy * dy + dx * dx)
        facing = (half_light[0] * dz + half_light[1] * dy + half_light[2] * dx) * inv
        shade_b[k + 2] = 0.5 + facing
        cz_b[k + 2] = dz
        cy_b[k + 2] = dy
        cx_b[k + 2] = dx
        inv_b[k + 2] = inv
        plus = jnp.log(1.0 + lax.exp2(here * (LOG2E / 8.0)))
        plus_b[k + 2] = plus
        return scale * plus

    def shade_up(k, depth):
        edge_b[k + 2] = depth
        return depth + shade(k)

    def shade_down(j, depth):
        k = -j
        depth = depth - shade(k)
        edge_b[k + 2] = depth
        return depth

    zero = jnp.zeros((ext, cols), jnp.float32)
    halo_arrived(1)
    run(1, 2 * step - 2, step - 1, blur, 0)
    far = run(2, 2 * step - 4, step - 2, shade_up, zero)
    for i in range(2, CHUNKS - 1):
        halo_arrived(i)
        run(step * i - 1, step, step, blur, 0)
        far = run(step * i - 2, step, step, shade_up, far)
    face.wait_recv()
    corner.wait_recv()
    run(-3, 4, 4, blur, 0)
    near = run(-1, 2, 2, shade_down, zero)
    run(1, 2, 2, shade_down, near)
    halo_arrived(CHUNKS - 1)
    run(slab - step - 1, step + 1, step + 1, blur, 0)
    smooth[slab + 3] = field[HALO + layer(slab - 1)]
    far = run(slab - step - 2, step + 2, step + 2, shade_up, far)

    toward = jnp.where(ascending, -1.0, 1.0)
    base = jnp.where(ascending, near, -far)
    depth = far - near

    def light_at(k):
        return lax.exp2(toward * edge_b[k + 2] + base)

    def composite(k, carry):
        left, m0, m1, m2, m3 = carry
        right = light_at(k + 1)
        here = smooth[k + 3]
        part = jnp.abs(left - right) * shade_b[k + 2]
        m0 = m0 + part
        part = part * here
        m1 = m1 + part
        part = part * here
        m2 = m2 + part
        part = part * here
        m3 = m3 + part
        edge_b[k + 2] = left
        return (right, m0, m1, m2, m3)

    edge_b[slab + 2] = far
    right, m0, m1, m2, m3 = run(0, slab, 8, composite, (light_at(0), zero, zero, zero, zero))
    edge_b[slab + 2] = right
    for c in range(3):
        mine[c] = coef_s[c, 0] * m0 + (coef_s[c, 1] / 8.0) * m1 + (coef_s[c, 2] / 64.0) * m2 + (coef_s[c, 3] / 512.0) * m3
    mine[3] = depth
    swap = across(mine, theirs, 2)
    swap.start()

    edge_b[0] = light_at(-2)
    edge_b[1] = light_at(-1)

    def bend(k, carry):
        inv = inv_b[k + 2]
        turn = (shade_b[k + 2] - 0.5) * inv
        cz_b[k + 2] = inv * (half_light[0] - turn * cz_b[k + 2])
        cy_b[k + 2] = inv * (half_light[1] - turn * cy_b[k + 2])
        cx_b[k + 2] = inv * (half_light[2] - turn * cx_b[k + 2])
        fac_b[k + 2] = slope * lax.exp2(smooth[k + 3] * (LOG2E / 8.0) - plus_b[k + 2] * LOG2E)
        return carry

    run(-2, slab, 8, bend, 0)
    run(slab - 2, 2, 2, bend, 0)
    enter0 = lax.exp2(-depth)
    swap.wait_recv()

    enter = jnp.where(ascending, lax.exp2(-theirs[3]), 1.0)
    row = lax.broadcasted_iota(jnp.int32, (ext, cols), 0)
    present = jnp.where(row < rows, 1.0, jnp.where(row < rows + HALO, has_next.astype(jnp.float32), has_prev.astype(jnp.float32)))
    present = present * float(depth_count)
    misfit = []
    before = zero
    for c in range(3):
        colour = jnp.where(ascending, theirs[c] + enter * mine[c], mine[c] + enter0 * theirs[c])
        colours[c] = colour[:rows]
        gap = (colour - info[2 + c]) * present
        misfit.append(gap)
        before = before + gap * jnp.where(ascending, mine[c], theirs[c])
    ramp_b[4] = jnp.where(ascending, enter, enter0) * before
    for i in range(4):
        ramp_b[i] = (
            enter * (misfit[0] * coef_s[0, i] + misfit[1] * coef_s[1, i] + misfit[2] * coef_s[2, i]) * (1.0 / 8.0**i)
        )
    share = rows // 2
    for c in range(3):
        image_v[c] = colours[c, pl.ds(pl.multiple_of(core * share, 8), share), :]

    face.wait_send()
    corner.wait_send()
    swap.wait_send()

    @pl.when(has_prev)
    def _():
        for i in range(CHUNKS + 1):
            halo_prev(i).wait_send()

    @pl.when(has_next)
    def _():
        for i in range(CHUNKS + 1):
            halo_next(i).wait_send()


def backward(
    smooth, shade_b, cz_b, cy_b, cx_b, fac_b, edge_b, ramp_b, image_v,
    image_out, grad_out,
    ay_b, qz_b, full_b, total, sems,
):
    slab, rows, cols = total.shape
    ext = rows + 2 * HALO
    step = slab // CHUNKS
    core = lax.axis_index("depth")
    sign = 2 * core - 1
    first = (1 - core) * (slab - 1)

    def chunk_start(i):
        return core * (step * i) + (1 - core) * (slab - step - step * i)

    def rx(value, shift):
        return pltpu.roll(value, shift % cols, 1)

    def ry(value, shift):
        return pltpu.roll(value, shift % ext, 0)

    image_copy = pltpu.make_async_copy(image_v, image_out, sems.at[CHUNKS])
    image_copy.start()
    ramp = [ramp_b[i] for i in range(4)]
    ramp2 = 2.0 * ramp[2]
    ramp3 = 3.0 * ramp[3]

    def pull(k, rest, down=False):
        left = edge_b[k + 2]
        signed = left - edge_b[k + 3]
        weight = jnp.abs(signed)
        here = smooth[k + 3]
        lit = shade_b[k + 2]
        value = ramp[0] + here * (ramp[1] + here * (ramp[2] + here * ramp[3]))
        deriv = ramp[1] + here * (ramp2 + here * ramp3)
        shown = lit * value
        pulled = weight * value
        if down:
            rest = rest + signed * shown
        direct = weight * lit * deriv + (left * shown - rest) * fac_b[k + 2]
        qx = pulled * cx_b[k + 2]
        qy = pulled * cy_b[k + 2]
        ay_b[k + 2] = (ry(qy, 1) - ry(qy, -1)) + (direct + rx(qx, 1) - rx(qx, -1))
        qz_b[k + 2] = pulled * cz_b[k + 2]
        return rest if down else rest - signed * shown

    def gather(k, carry):
        full_b[k + 1] = ay_b[k + 2] + qz_b[k + 1] - qz_b[k + 3]
        return carry

    def spread(k, carry):
        here = full_b[k + 1]
        mid = here[:rows]
        around = 2.0 * mid + full_b[k, pl.ds(0, rows), :] + full_b[k + 2, pl.ds(0, rows), :]
        around = around + (ry(here, 1) + ry(here, -1))[:rows] + (rx(mid, 1) + rx(mid, -1))
        total[first + sign * k] = around
        return carry

    outs = []

    def write(i):
        start = chunk_start(i)
        out = pltpu.make_async_copy(total.at[pl.ds(start, step)], grad_out.at[pl.ds(start, step)], sems.at[i])
        out.start()
        outs.append(out)

    rest = ramp_b[4]
    pull(-2, pull(-1, rest, True), True)
    qz_b[slab + 2] = jnp.zeros((ext, cols), jnp.float32)
    rest = run(0, 2, 2, pull, rest)
    run(-1, 2, 2, gather, 0)
    for i in range(CHUNKS - 1):
        rest = run(step * i + 2, step, step, pull, rest)
        run(step * i + 1, step, step, gather, 0)
        run(step * i, step, step, spread, 0)
        write(i)
    run(slab - step + 2, step - 2, step - 2, pull, rest)
    run(slab - step + 1, step - 1, step - 1, gather, 0)
    full_b[slab + 1] = qz_b[slab + 1]
    run(slab - step, step, step, spread, 0)
    write(CHUNKS - 1)
    image_copy.wait()
    for out in outs:
        out.wait()


def solution(mesh):
    tiles = mesh.shape["tile"]

    def shards(density, absorption, view_dir, target_ids, palette, coef, light):
        slab, rows, cols = density.shape
        ext = rows + 2 * HALO
        f32 = jnp.float32
        cells = (slab + 2, ext, cols)
        scratch = [
            pltpu.VMEM((slab + 2 * HALO, ext, cols), f32),
            pltpu.VMEM((5, ext, cols), f32),
            pltpu.VMEM(cells, f32),
            pltpu.VMEM(cells, f32),
            pltpu.VMEM(target_ids.shape, jnp.int32),
            pltpu.VMEM(palette.shape, f32),
            pltpu.SMEM(view_dir.shape, jnp.int32),
            pltpu.SMEM(coef.shape, f32),
            pltpu.SMEM(light.shape, f32),
            pltpu.VMEM((4, ext, cols), f32),
            pltpu.VMEM((4, ext, cols), f32),
            pltpu.VMEM((3, rows, cols), f32),
            pltpu.SemaphoreType.DMA,
            pltpu.SemaphoreType.DMA((6,)),
            pltpu.SemaphoreType.DMA((2, CHUNKS + 1)),
            pltpu.SemaphoreType.DMA((2, CHUNKS + 1)),
            pltpu.SemaphoreType.DMA((3,)),
            pltpu.SemaphoreType.DMA((3,)),
        ]
        args = (density, absorption, view_dir, target_ids, palette, coef, light)
        fields = pl.pallas_call(
            functools.partial(forward, tiles, slab, rows, cols, 2 * slab),
            out_shape=(
                pltpu.VMEM((slab + 4, ext, cols), f32),
                *[pltpu.VMEM(cells, f32)] * 5,
                pltpu.VMEM((slab + 3, ext, cols), f32),
                pltpu.VMEM((5, ext, cols), f32),
                pltpu.VMEM((3, rows // 2, cols), f32),
            ),
            in_specs=[pl.BlockSpec(memory_space=pl.ANY)] * 7,
            out_specs=[pl.BlockSpec(memory_space=pltpu.VMEM)] * 9,
            scratch_shapes=scratch,
            compiler_params=pltpu.CompilerParams(
                collective_id=0, has_side_effects=True, vmem_limit_bytes=16 * 1024 * 1024
            ),
        )(*[pltpu.with_memory_space_constraint(x, pltpu.HBM) for x in args])
        return pl.pallas_call(
            backward,
            out_shape=(jax.ShapeDtypeStruct((3, rows // 2, cols), f32), jax.ShapeDtypeStruct(density.shape, f32)),
            in_specs=[pl.BlockSpec(memory_space=pltpu.VMEM)] * 9,
            out_specs=[pl.BlockSpec(memory_space=pl.ANY)] * 2,
            scratch_shapes=[
                pltpu.VMEM(cells, f32),
                pltpu.VMEM((slab + 3, ext, cols), f32),
                pltpu.VMEM((slab + 2, ext, cols), f32),
                pltpu.VMEM(density.shape, f32),
                pltpu.SemaphoreType.DMA((CHUNKS + 1,)),
            ],
            compiler_params=pltpu.CompilerParams(vmem_limit_bytes=16 * 1024 * 1024),
        )(*fields)

    placed = (P("depth", "tile", None), P("tile", None), P("tile"), P("tile", None), P(), P(), P())
    return jax.shard_map(
        shards,
        mesh=mesh,
        in_specs=placed,
        out_specs=(P(None, ("tile", "depth"), None), P("depth", "tile", None)),
        check_vma=False,
    )
```

time: 23.2 us -> 19.1 us (0.82)
  the two profiles are of different devices: /device:TPU:257 before, /device:TPU:1 now
where the time goes in v4:
time: 19.1 us; the launch traced here: 19 us
  Pallas kernels  18.3 us (96%)
  between operations  0.64 us (3%)
    pallas_call x1, Pallas kernels, shards(): pl.pallas_call(functools.partial(forward, tiles, slab, rows, cols, 2 * sl...  16.2 us
    pallas_call x1, Pallas kernels, shards(): pl.pallas_call(backward, out_shape=(jax.ShapeDtypeStruct((3, rows // 2, c...  2.13 us

profile of v4, /device:TPU:1, one launch (start us, length us, event | category | flops | bytes accessed | tf_op | source)
XLA Modules:
  0.0 19.0 jit_solution(15534322637357805372)
XLA Ops:
  0.6 16.2 %shard_map.86 = (f32[36,24,256]{2,1,0:T(8,128)S(1)}, f32[34,24,256]{2,1,0:T(8,128)S(1)}, f32[34,24,256]{2,1,0:T(8,128)S(1)}, f32[34,24,256]{2,1,0:T(8,128)S(1)},...) custom-call(f32[32,16,256]{2,1,0:T(8,128)} %density.1, ...), custom_call_target="tpu_custom_call" | custom-call | tf_op jit(solution)/shard_map/pallas_call | solution.py:448
  16.8 2.1 %shard_map.87 = (f32[3,8,256]{2,1,0:T(8,128)}, f32[32,16,256]{2,1,0:T(8,128)}) custom-call(f32[36,24,256]{2,1,0:T(8,128)S(1)} %get-tuple-element.11.smooth, f32[34,24,256]{2,1,0:T(8,128)S(1)} %get-tuple-element.12.shade_b, f32[34,24,256]{2,1,0:T(8,128)S(1)} %get-tuple-element.13.cz_b, f32[34,24,256]{2,1,0:T(8,128)S(1)} %get-tuple-element.14.cy_b, ...), custom_call_target="tpu_custom_call" | custom-call | tf_op jit(solution)/shard_map/pallas_call | solution.py:464

commit v5 on v4

--- a/solution.py
+++ b/solution.py
@@ -10,7 +10,9 @@
 
 MESH = pl.DeviceIdType.MESH
 LOG2E = math.log2(math.e)
-CHUNKS = 4
+CUTS = (0, 4, 12, 20, 28, 32)
+CHUNKS = len(CUTS) - 1
+PARTS = 4
 HALO = 4
 
 
@@ -23,11 +25,23 @@
     return lax.fori_loop(0, count // unroll, several, carry)
 
 
+def grouped(layers, group, one, carry):
+    layers = list(layers)
+    for at in range(0, len(layers), group):
+        stores = []
+        for k in layers[at : at + group]:
+            carry, more = one(k, carry)
+            stores += more
+        for ref, index, value in stores:
+            ref[index] = value
+    return carry
+
+
 def forward(
     tiles, slab, rows, cols, depth_count,
     density, absorption, view_dir, target_ids, palette, coef, light,
-    smooth, shade_b, cz_b, cy_b, cx_b, fac_b, edge_b, ramp_b, image_v,
-    field, info, plus_b, inv_b, ids_v, pal_v, view_s, coef_s, light_s, mine, theirs, colours,
+    smooth, shade_b, cz_b, cy_b, cx_b, fac_b, gain_b, ramp_b, image_v,
+    field, info, edge_b, plus_b, inv_b, ids_v, pal_v, view_s, coef_s, light_s, mine, theirs, colours,
     load_sem, small_sem, halo_send, halo_recv, core_send, core_recv,
 ):
     tile = lax.axis_index("tile")
@@ -36,15 +50,15 @@
     has_prev = tile > 0
     has_next = tile < tiles - 1
     ext = rows + 2 * HALO
-    step = slab // CHUNKS
+    cuts = [slab * cut // 32 for cut in CUTS]
     sign = 2 * core - 1
     first = (1 - core) * (slab - 1)
 
     def layer(k):
         return first + sign * k
 
-    def chunk_start(i):
-        return core * (step * i) + other * (slab - step - step * i)
+    def chunk(i):
+        return core * cuts[i] + other * (slab - cuts[i + 1]), cuts[i + 1] - cuts[i]
 
     prev_id = (jnp.maximum(tile - 1, 0), core)
     next_id = (jnp.minimum(tile + 1, tiles - 1), core)
@@ -137,13 +151,13 @@
     def halo_prev(i):
         if i == CHUNKS:
             return to_prev(info.at[:, low, :], info.at[:, after, :], i)
-        start = chunk_start(i)
+        start, step = chunk(i)
         return to_prev(density.at[pl.ds(start, step), low, :], field.at[pl.ds(HALO + start, step), after, :], i)
 
     def halo_next(i):
         if i == CHUNKS:
             return to_next(info.at[:, high, :], info.at[:, before_rows, :], i)
-        start = chunk_start(i)
+        start, step = chunk(i)
         return to_next(density.at[pl.ds(start, step), high, :], field.at[pl.ds(HALO + start, step), before_rows, :], i)
 
     def halo_start(i):
@@ -166,7 +180,7 @@
 
     halo_start(0)
     face.start()
-    for i in range(1, CHUNKS):
+    for i in range(1, CHUNKS - 2):
         halo_start(i)
 
     for copy in smalls:
@@ -182,25 +196,20 @@
             for x in range(0, cols, 128):
                 picked = jnp.take_along_axis(table, ids_v[pl.ds(y, 8), pl.ds(x, 128)], axis=1, mode="promise_in_bounds")
                 info[2 + c, pl.ds(y, 8), pl.ds(x, 128)] = picked
-    halo_start(CHUNKS)
+    for i in (CHUNKS, CHUNKS - 2, CHUNKS - 1):
+        halo_start(i)
     half_light = [0.5 * light_s[0] * sign.astype(jnp.float32), 0.5 * light_s[1], 0.5 * light_s[2]]
 
     own.wait()
     halo_arrived(0)
     corner.start()
-    halo_arrived(CHUNKS)
-    absorb = info[0]
-    ascending = info[1] == other.astype(jnp.float32)
-    scale = absorb * (LOG2E / depth_count)
-    slope = absorb * (1.0 / (8.0 * depth_count))
 
     def blur(k, carry):
         at = HALO + layer(k)
         here = field[at]
         total = 2.0 * here + field[at - 1] + field[at + 1]
         total = total + (ry(here, 1) + ry(here, -1)) + (rx(here, 1) + rx(here, -1))
-        smooth[k + 3] = total
-        return carry
+        return carry, [(smooth, k + 3, total)]
 
     def shade(k):
         here = smooth[k + 3]
@@ -209,88 +218,108 @@
         dx = rx(here, -1) - rx(here, 1)
         inv = lax.rsqrt(256.0 + dz * dz + dy * dy + dx * dx)
         facing = (half_light[0] * dz + half_light[1] * dy + half_light[2] * dx) * inv
-        shade_b[k + 2] = 0.5 + facing
-        cz_b[k + 2] = dz
-        cy_b[k + 2] = dy
-        cx_b[k + 2] = dx
-        inv_b[k + 2] = inv
         plus = jnp.log(1.0 + lax.exp2(here * (LOG2E / 8.0)))
-        plus_b[k + 2] = plus
-        return scale * plus
+        at = k + 2
+        return plus, [
+            (shade_b, at, 0.5 + facing), (cz_b, at, dz), (cy_b, at, dy), (cx_b, at, dx), (inv_b, at, inv), (plus_b, at, plus)
+        ]
 
     def shade_up(k, depth):
-        edge_b[k + 2] = depth
-        return depth + shade(k)
-
-    def shade_down(j, depth):
-        k = -j
-        depth = depth - shade(k)
-        edge_b[k + 2] = depth
-        return depth
+        plus, stores = shade(k)
+        return depth + plus, [(edge_b, k + 2, depth), *stores]
+
+    def shade_down(k, depth):
+        plus, stores = shade(k)
+        return depth - plus, [(edge_b, k + 2, depth - plus), *stores]
 
     zero = jnp.zeros((ext, cols), jnp.float32)
-    halo_arrived(1)
-    run(1, 2 * step - 2, step - 1, blur, 0)
-    far = run(2, 2 * step - 4, step - 2, shade_up, zero)
-    for i in range(2, CHUNKS - 1):
+    def composite(lo, hi, toward, base, sums):
+        left = lax.exp2(toward * edge_b[lo + 2] + base)
+        m0, m1, m2, m3 = sums
+        for k in range(lo, hi):
+            right = lax.exp2(toward * edge_b[k + 3] + base)
+            here = smooth[k + 3]
+            part = jnp.abs(left - right) * shade_b[k + 2]
+            m0 = m0 + part
+            part = part * here
+            m1 = m1 + part
+            part = part * here
+            m2 = m2 + part
+            part = part * here
+            m3 = m3 + part
+            left = right
+        return m0, m1, m2, m3
+
+    def composite_more(lo, hi, start, end, sums):
+        dim = jnp.where(ascending, 1.0, lax.exp2((start - end) * scale))
+        edge_b[hi + 2] = end
+        return composite(lo, hi, toward, jnp.where(ascending, 0.0, -end) * scale, [m * dim for m in sums])
+
+    far = zero
+    blurred, shaded, summed = 1, 2, 2
+    start = zero
+    sums = [zero] * 4
+    for i in range(1, CHUNKS):
+        last = i == CHUNKS - 1
+        if last:
+            face.wait_recv()
+            corner.wait_recv()
+            grouped((0, -1, -2, -3), 4, blur, 0)
+            near = grouped((1, 0), 2, shade_down, zero)
+            grouped((-1, -2), 2, shade_down, near)
+            near_sums = composite(0, 2, toward, jnp.where(ascending, near, 0.0) * scale, [zero] * 4)
         halo_arrived(i)
-        run(step * i - 1, step, step, blur, 0)
-        far = run(step * i - 2, step, step, shade_up, far)
-    face.wait_recv()
-    corner.wait_recv()
-    run(-3, 4, 4, blur, 0)
-    near = run(-1, 2, 2, shade_down, zero)
-    run(1, 2, 2, shade_down, near)
-    halo_arrived(CHUNKS - 1)
-    run(slab - step - 1, step + 1, step + 1, blur, 0)
-    smooth[slab + 3] = field[HALO + layer(slab - 1)]
-    far = run(slab - step - 2, step + 2, step + 2, shade_up, far)
-
-    toward = jnp.where(ascending, -1.0, 1.0)
-    base = jnp.where(ascending, near, -far)
-    depth = far - near
-
-    def light_at(k):
-        return lax.exp2(toward * edge_b[k + 2] + base)
-
-    def composite(k, carry):
-        left, m0, m1, m2, m3 = carry
-        right = light_at(k + 1)
-        here = smooth[k + 3]
-        part = jnp.abs(left - right) * shade_b[k + 2]
-        m0 = m0 + part
-        part = part * here
-        m1 = m1 + part
-        part = part * here
-        m2 = m2 + part
-        part = part * here
-        m3 = m3 + part
-        edge_b[k + 2] = left
-        return (right, m0, m1, m2, m3)
-
-    edge_b[slab + 2] = far
-    right, m0, m1, m2, m3 = run(0, slab, 8, composite, (light_at(0), zero, zero, zero, zero))
-    edge_b[slab + 2] = right
+        reach = slab if last else cuts[i + 1] - 1
+        grouped(range(blurred, reach), 4, blur, 0)
+        if last:
+            smooth[slab + 3] = field[HALO + layer(slab - 1)]
+        blurred = reach
+        reach = slab if last else reach - 1
+        far = grouped(range(shaded, reach), 2, shade_up, far)
+        shaded = reach
+        if i == CHUNKS - 3:
+            halo_arrived(CHUNKS)
+            absorb = info[0]
+            ascending = info[1] == other.astype(jnp.float32)
+            scale = absorb * (LOG2E / depth_count)
+            slope = absorb * (1.0 / (8.0 * depth_count))
+            toward = jnp.where(ascending, -scale, scale)
+        if i >= CHUNKS - 3:
+            sums = composite_more(summed, shaded, start, far, sums)
+            summed, start = shaded, far
+
+    near_dim = jnp.where(ascending, 1.0, lax.exp2(-far * scale))
+    far_dim = jnp.where(ascending, lax.exp2(near * scale), 1.0)
+    m0, m1, m2, m3 = [near_dim * m + far_dim * n for m, n in zip(near_sums, sums)]
+    base = jnp.where(ascending, near, -far) * scale
+    depth = (far - near) * scale
     for c in range(3):
         mine[c] = coef_s[c, 0] * m0 + (coef_s[c, 1] / 8.0) * m1 + (coef_s[c, 2] / 64.0) * m2 + (coef_s[c, 3] / 512.0) * m3
     mine[3] = depth
     swap = across(mine, theirs, 2)
     swap.start()
 
-    edge_b[0] = light_at(-2)
-    edge_b[1] = light_at(-1)
-
-    def bend(k, carry):
+    side = jnp.where(ascending, 1.0, -1.0)
+    slope = side * slope
+
+    def bend(k, left):
+        right = lax.exp2(toward * edge_b[k + 3] + base)
+        weight = jnp.abs(left - right)
+        lit = shade_b[k + 2]
         inv = inv_b[k + 2]
-        turn = (shade_b[k + 2] - 0.5) * inv
-        cz_b[k + 2] = inv * (half_light[0] - turn * cz_b[k + 2])
-        cy_b[k + 2] = inv * (half_light[1] - turn * cy_b[k + 2])
-        cx_b[k + 2] = inv * (half_light[2] - turn * cx_b[k + 2])
-        fac_b[k + 2] = slope * lax.exp2(smooth[k + 3] * (LOG2E / 8.0) - plus_b[k + 2] * LOG2E)
-        return carry
-
-    run(-2, slab, 8, bend, 0)
-    run(slab - 2, 2, 2, bend, 0)
+        turn = (lit - 0.5) * inv
+        bright = weight * inv
+        cz_b[k + 2] = bright * (half_light[0] - turn * cz_b[k + 2])
+        cy_b[k + 2] = bright * (half_light[1] - turn * cy_b[k + 2])
+        cx_b[k + 2] = bright * (half_light[2] - turn * cx_b[k + 2])
+        fac = slope * lax.exp2(smooth[k + 3] * (LOG2E / 8.0) - plus_b[k + 2] * LOG2E)
+        fac_b[k + 2] = fac
+        gain_b[k + 2] = side * (left * lit) * fac
+        shade_b[k + 2] = weight * lit
+        return right
+
+    left = run(-2, slab, 8, bend, lax.exp2(toward * edge_b[0] + base))
+    run(slab - 2, 2, 2, bend, left)
     enter0 = lax.exp2(-depth)
     swap.wait_recv()
 
@@ -306,7 +335,7 @@
         gap = (colour - info[2 + c]) * present
         misfit.append(gap)
         before = before + gap * jnp.where(ascending, mine[c], theirs[c])
-    ramp_b[4] = jnp.where(ascending, enter, enter0) * before
+    ramp_b[4] = jnp.where(ascending, enter, -enter0) * before
     for i in range(4):
         ramp_b[i] = (
             enter * (misfit[0] * coef_s[0, i] + misfit[1] * coef_s[1, i] + misfit[2] * coef_s[2, i]) * (1.0 / 8.0**i)
@@ -331,13 +360,13 @@
 
 
 def backward(
-    smooth, shade_b, cz_b, cy_b, cx_b, fac_b, edge_b, ramp_b, image_v,
+    smooth, lit_b, cz_b, cy_b, cx_b, fac_b, gain_b, ramp_b, image_v,
     image_out, grad_out,
     ay_b, qz_b, full_b, total, sems,
 ):
     slab, rows, cols = total.shape
     ext = rows + 2 * HALO
-    step = slab // CHUNKS
+    step = slab // PARTS
     core = lax.axis_index("depth")
     sign = 2 * core - 1
     first = (1 - core) * (slab - 1)
@@ -351,42 +380,41 @@
     def ry(value, shift):
         return pltpu.roll(value, shift % ext, 0)
 
-    image_copy = pltpu.make_async_copy(image_v, image_out, sems.at[CHUNKS])
+    image_copy = pltpu.make_async_copy(image_v, image_out, sems.at[PARTS])
     image_copy.start()
     ramp = [ramp_b[i] for i in range(4)]
     ramp2 = 2.0 * ramp[2]
     ramp3 = 3.0 * ramp[3]
 
     def pull(k, rest, down=False):
-        left = edge_b[k + 2]
-        signed = left - edge_b[k + 3]
-        weight = jnp.abs(signed)
         here = smooth[k + 3]
-        lit = shade_b[k + 2]
+        lit = lit_b[k + 2]
         value = ramp[0] + here * (ramp[1] + here * (ramp[2] + here * ramp[3]))
         deriv = ramp[1] + here * (ramp2 + here * ramp3)
         shown = lit * value
-        pulled = weight * value
         if down:
-            rest = rest + signed * shown
-        direct = weight * lit * deriv + (left * shown - rest) * fac_b[k + 2]
-        qx = pulled * cx_b[k + 2]
-        qy = pulled * cy_b[k + 2]
-        ay_b[k + 2] = (ry(qy, 1) - ry(qy, -1)) + (direct + rx(qx, 1) - rx(qx, -1))
-        qz_b[k + 2] = pulled * cz_b[k + 2]
-        return rest if down else rest - signed * shown
+            rest = rest + shown
+        direct = lit * deriv + (gain_b[k + 2] * value - rest * fac_b[k + 2])
+        qx = value * cx_b[k + 2]
+        qy = value * cy_b[k + 2]
+        stores = [
+            (ay_b, k + 2, (ry(qy, 1) - ry(qy, -1)) + (direct + rx(qx, 1) - rx(qx, -1))),
+            (qz_b, k + 2, value * cz_b[k + 2]),
+        ]
+        return rest if down else rest - shown, stores
+
+    def pull_down(k, rest):
+        return pull(k, rest, True)
 
     def gather(k, carry):
-        full_b[k + 1] = ay_b[k + 2] + qz_b[k + 1] - qz_b[k + 3]
-        return carry
+        return carry, [(full_b, k + 1, ay_b[k + 2] + qz_b[k + 1] - qz_b[k + 3])]
 
     def spread(k, carry):
         here = full_b[k + 1]
         mid = here[:rows]
         around = 2.0 * mid + full_b[k, pl.ds(0, rows), :] + full_b[k + 2, pl.ds(0, rows), :]
         around = around + (ry(here, 1) + ry(here, -1))[:rows] + (rx(mid, 1) + rx(mid, -1))
-        total[first + sign * k] = around
-        return carry
+        return carry, [(total, first + sign * k, around)]
 
     outs = []
 
@@ -397,20 +425,19 @@
         outs.append(out)
 
     rest = ramp_b[4]
-    pull(-2, pull(-1, rest, True), True)
+    grouped((-1, -2), 2, pull_down, rest)
     qz_b[slab + 2] = jnp.zeros((ext, cols), jnp.float32)
-    rest = run(0, 2, 2, pull, rest)
-    run(-1, 2, 2, gather, 0)
-    for i in range(CHUNKS - 1):
-        rest = run(step * i + 2, step, step, pull, rest)
-        run(step * i + 1, step, step, gather, 0)
-        run(step * i, step, step, spread, 0)
+    done = 0
+    for i in range(PARTS):
+        last = i == PARTS - 1
+        reach = slab if last else step * (i + 1) + 2
+        rest = grouped(range(done, reach), 2, pull, rest)
+        grouped(range(done - 1, slab if last else reach - 1), 4, gather, 0)
+        done = reach
+        if last:
+            full_b[slab + 1] = qz_b[slab + 1]
+        grouped(range(step * i, step * (i + 1)), 4, spread, 0)
         write(i)
-    run(slab - step + 2, step - 2, step - 2, pull, rest)
-    run(slab - step + 1, step - 1, step - 1, gather, 0)
-    full_b[slab + 1] = qz_b[slab + 1]
-    run(slab - step, step, step, spread, 0)
-    write(CHUNKS - 1)
     image_copy.wait()
     for out in outs:
         out.wait()
@@ -427,6 +454,7 @@
         scratch = [
             pltpu.VMEM((slab + 2 * HALO, ext, cols), f32),
             pltpu.VMEM((5, ext, cols), f32),
+            pltpu.VMEM((slab + 3, ext, cols), f32),
             pltpu.VMEM(cells, f32),
             pltpu.VMEM(cells, f32),
             pltpu.VMEM(target_ids.shape, jnp.int32),
@@ -449,8 +477,7 @@
             functools.partial(forward, tiles, slab, rows, cols, 2 * slab),
             out_shape=(
                 pltpu.VMEM((slab + 4, ext, cols), f32),
-                *[pltpu.VMEM(cells, f32)] * 5,
-                pltpu.VMEM((slab + 3, ext, cols), f32),
+                *[pltpu.VMEM(cells, f32)] * 6,
                 pltpu.VMEM((5, ext, cols), f32),
                 pltpu.VMEM((3, rows // 2, cols), f32),
             ),
@@ -471,7 +498,7 @@
                 pltpu.VMEM((slab + 3, ext, cols), f32),
                 pltpu.VMEM((slab + 2, ext, cols), f32),
                 pltpu.VMEM(density.shape, f32),
-                pltpu.SemaphoreType.DMA((CHUNKS + 1,)),
+                pltpu.SemaphoreType.DMA((PARTS + 1,)),
             ],
             compiler_params=pltpu.CompilerParams(vmem_limit_bytes=16 * 1024 * 1024),
         )(*fields)

time: 19.1 us -> 17.7 us (0.927)
  Pallas kernels: 18.3 us -> 16.9 us
    pallas_call x1, Pallas kernels: 16.2 us -> 15 us  [shards(): pl.pallas_call(functools.partial(forward, tiles, slab, rows, cols, 2 * sl...]
    pallas_call x1, Pallas kernels: 2.13 us -> 1.9 us  [shards(): pl.pallas_call(backward, out_shape=(jax.ShapeDtypeStruct((3, rows // 2, c...]
where the time goes in v5:
time: 17.7 us; the launch traced here: 17.6 us
  Pallas kernels  16.9 us (95%)
  between operations  0.64 us (4%)
    pallas_call x1, Pallas kernels, shards(): pl.pallas_call(functools.partial(forward, tiles, slab, rows, cols, 2 * sl...  15 us
    pallas_call x1, Pallas kernels, shards(): pl.pallas_call(backward, out_shape=(jax.ShapeDtypeStruct((3, rows // 2, c...  1.9 us

profile of v5, /device:TPU:1, one launch (start us, length us, event | category | flops | bytes accessed | tf_op | source)
XLA Modules:
  0.0 17.6 jit_solution(6699951696547879136)
XLA Ops:
  0.6 15.0 %shard_map.86 = (f32[36,24,256]{2,1,0:T(8,128)S(1)}, f32[34,24,256]{2,1,0:T(8,128)S(1)}, f32[34,24,256]{2,1,0:T(8,128)S(1)}, f32[34,24,256]{2,1,0:T(8,128)S(1)},...) custom-call(f32[32,16,256]{2,1,0:T(8,128)} %density.1, ...), custom_call_target="tpu_custom_call" | custom-call | tf_op jit(solution)/shard_map/pallas_call | solution.py:476
  15.7 1.9 %shard_map.87 = (f32[3,8,256]{2,1,0:T(8,128)}, f32[32,16,256]{2,1,0:T(8,128)}) custom-call(f32[36,24,256]{2,1,0:T(8,128)S(1)} %get-tuple-element.11.smooth, f32[34,24,256]{2,1,0:T(8,128)S(1)} %get-tuple-element.12.lit_b, f32[34,24,256]{2,1,0:T(8,128)S(1)} %get-tuple-element.13.cz_b, f32[34,24,256]{2,1,0:T(8,128)S(1)} %get-tuple-element.14.cy_b, ...), custom_call_target="tpu_custom_call" | custom-call | tf_op jit(solution)/shard_map/pallas_call | solution.py:491

commit v6 on v5

--- a/solution.py
+++ b/solution.py
@@ -10,7 +10,7 @@
 
 MESH = pl.DeviceIdType.MESH
 LOG2E = math.log2(math.e)
-CUTS = (0, 4, 12, 20, 28, 32)
+CUTS = (0, 8, 14, 20, 26, 32)
 CHUNKS = len(CUTS) - 1
 PARTS = 4
 HALO = 4
@@ -201,8 +201,6 @@
     half_light = [0.5 * light_s[0] * sign.astype(jnp.float32), 0.5 * light_s[1], 0.5 * light_s[2]]
 
     own.wait()
-    halo_arrived(0)
-    corner.start()
 
     def blur(k, carry):
         at = HALO + layer(k)
@@ -210,6 +208,37 @@
         total = 2.0 * here + field[at - 1] + field[at + 1]
         total = total + (ry(here, 1) + ry(here, -1)) + (rx(here, 1) + rx(here, -1))
         return carry, [(smooth, k + 3, total)]
+
+    row8 = lax.broadcasted_iota(jnp.int32, (8, cols), 0)
+
+    def blur_own(k, carry):
+        at = HALO + layer(k)
+        here = field[at, pl.ds(0, rows), :]
+        tops = [pltpu.roll(here[y : y + 8], 1, 0) for y in range(0, rows, 8)]
+        ends = [pltpu.roll(here[y : y + 8], 7, 0) for y in range(0, rows, 8)]
+        none = jnp.zeros((8, cols), jnp.float32)
+        up = [jnp.where(row8 < 1, before, now) for before, now in zip([none, *tops[:-1]], tops)]
+        down = [jnp.where(row8 > 6, after_, now) for after_, now in zip([*ends[1:], none], ends)]
+        total = 2.0 * here + field[at - 1, pl.ds(0, rows), :] + field[at + 1, pl.ds(0, rows), :]
+        total = total + (rx(here, 1) + rx(here, -1)) + (jnp.concatenate(up, 0) + jnp.concatenate(down, 0))
+        return carry, [(smooth, (k + 3, pl.ds(0, rows), slice(None)), total)]
+
+    def blur_halo(k, carry):
+        at = HALO + layer(k)
+        halo = pl.ds(rows, 2 * HALO)
+        here = field[at, halo, :]
+        top = pltpu.roll(here, 1, 0)
+        end = pltpu.roll(here, 7, 0)
+        up = jnp.where(row8 < 1, pltpu.roll(field[at, pl.ds(rows - 8, 8), :], 1, 0), top)
+        down = jnp.where(row8 > 6, pltpu.roll(field[at, pl.ds(0, 8), :], 7, 0), end)
+        total = 2.0 * here + field[at - 1, halo, :] + field[at + 1, halo, :]
+        total = total + (rx(here, 1) + rx(here, -1)) + (up + down)
+        low_rows, high_rows = (k + 3, pl.ds(0, 8), slice(None)), (k + 3, pl.ds(rows - 8, 8), slice(None))
+        return carry, [
+            (smooth, (k + 3, halo, slice(None)), total),
+            (smooth, low_rows, smooth[low_rows] + jnp.where(row8 < 1, top, 0.0)),
+            (smooth, high_rows, smooth[high_rows] + jnp.where(row8 > 6, end, 0.0)),
+        ]
 
     def shade(k):
         here = smooth[k + 3]
@@ -234,21 +263,25 @@
 
     zero = jnp.zeros((ext, cols), jnp.float32)
     def composite(lo, hi, toward, base, sums):
-        left = lax.exp2(toward * edge_b[lo + 2] + base)
-        m0, m1, m2, m3 = sums
-        for k in range(lo, hi):
-            right = lax.exp2(toward * edge_b[k + 3] + base)
-            here = smooth[k + 3]
-            part = jnp.abs(left - right) * shade_b[k + 2]
-            m0 = m0 + part
-            part = part * here
-            m1 = m1 + part
-            part = part * here
-            m2 = m2 + part
-            part = part * here
-            m3 = m3 + part
-            left = right
-        return m0, m1, m2, m3
+        parts = []
+        for y in range(0, ext, 8):
+            tile_rows = pl.ds(y, 8)
+            way, from_, (m0, m1, m2, m3) = toward[y : y + 8], base[y : y + 8], [m[y : y + 8] for m in sums]
+            left = lax.exp2(way * edge_b[lo + 2, tile_rows, :] + from_)
+            for k in range(lo, hi):
+                right = lax.exp2(way * edge_b[k + 3, tile_rows, :] + from_)
+                here = smooth[k + 3, tile_rows, :]
+                part = jnp.abs(left - right) * shade_b[k + 2, tile_rows, :]
+                m0 = m0 + part
+                part = part * here
+                m1 = m1 + part
+                part = part * here
+                m2 = m2 + part
+                part = part * here
+                m3 = m3 + part
+                left = right
+            parts.append((m0, m1, m2, m3))
+        return [jnp.concatenate([part[j] for part in parts], 0) for j in range(4)]
 
     def composite_more(lo, hi, start, end, sums):
         dim = jnp.where(ascending, 1.0, lax.exp2((start - end) * scale))
@@ -259,7 +292,8 @@
     blurred, shaded, summed = 1, 2, 2
     start = zero
     sums = [zero] * 4
-    for i in range(1, CHUNKS):
+    grouped(range(1, slab), 4, blur_own, 0)
+    for i in range(CHUNKS):
         last = i == CHUNKS - 1
         if last:
             face.wait_recv()
@@ -269,8 +303,10 @@
             grouped((-1, -2), 2, shade_down, near)
             near_sums = composite(0, 2, toward, jnp.where(ascending, near, 0.0) * scale, [zero] * 4)
         halo_arrived(i)
+        if i == 0:
+            corner.start()
         reach = slab if last else cuts[i + 1] - 1
-        grouped(range(blurred, reach), 4, blur, 0)
+        grouped(range(blurred, reach), 4, blur_halo, 0)
         if last:
             smooth[slab + 3] = field[HALO + layer(slab - 1)]
         blurred = reach
@@ -302,24 +338,29 @@
     side = jnp.where(ascending, 1.0, -1.0)
     slope = side * slope
 
-    def bend(k, left):
-        right = lax.exp2(toward * edge_b[k + 3] + base)
-        weight = jnp.abs(left - right)
-        lit = shade_b[k + 2]
-        inv = inv_b[k + 2]
-        turn = (lit - 0.5) * inv
-        bright = weight * inv
-        cz_b[k + 2] = bright * (half_light[0] - turn * cz_b[k + 2])
-        cy_b[k + 2] = bright * (half_light[1] - turn * cy_b[k + 2])
-        cx_b[k + 2] = bright * (half_light[2] - turn * cx_b[k + 2])
-        fac = slope * lax.exp2(smooth[k + 3] * (LOG2E / 8.0) - plus_b[k + 2] * LOG2E)
-        fac_b[k + 2] = fac
-        gain_b[k + 2] = side * (left * lit) * fac
-        shade_b[k + 2] = weight * lit
-        return right
-
-    left = run(-2, slab, 8, bend, lax.exp2(toward * edge_b[0] + base))
-    run(slab - 2, 2, 2, bend, left)
+    for y in range(0, ext, 8):
+        tile_rows = pl.ds(y, 8)
+        way, from_, slope_y, side_y = toward[y : y + 8], base[y : y + 8], slope[y : y + 8], side[y : y + 8]
+
+        def bend(k, left, tile_rows=tile_rows, way=way, from_=from_, slope_y=slope_y, side_y=side_y):
+            right = lax.exp2(way * edge_b[k + 3, tile_rows, :] + from_)
+            cell = (k + 2, tile_rows, slice(None))
+            weight = jnp.abs(left - right)
+            lit = shade_b[cell]
+            inv = inv_b[cell]
+            turn = (lit - 0.5) * inv
+            bright = weight * inv
+            cz_b[cell] = bright * (half_light[0] - turn * cz_b[cell])
+            cy_b[cell] = bright * (half_light[1] - turn * cy_b[cell])
+            cx_b[cell] = bright * (half_light[2] - turn * cx_b[cell])
+            fac = slope_y * lax.exp2(smooth[k + 3, tile_rows, :] * (LOG2E / 8.0) - plus_b[cell] * LOG2E)
+            fac_b[cell] = fac
+            gain_b[cell] = side_y * (left * lit) * fac
+            shade_b[cell] = weight * lit
+            return right
+
+        left = run(-2, slab, 16, bend, lax.exp2(way * edge_b[0, tile_rows, :] + from_))
+        run(slab - 2, 2, 2, bend, left)
     enter0 = lax.exp2(-depth)
     swap.wait_recv()
 
@@ -359,10 +400,30 @@
             halo_next(i).wait_send()
 
 
+def lay(ref, at, value):
+    rows, cols = value.shape[0] - 8, value.shape[1]
+    stores = []
+    for h in range(cols // 128):
+        lanes = value[:, 128 * h : 128 * h + 128]
+        stores.append((ref, (at, h, pl.ds(8, rows), slice(None)), lanes[:rows]))
+        stores.append((ref, (at, h, pl.ds(0, 8), slice(None)), lanes[rows:]))
+        stores.append((ref, (at, h, pl.ds(rows + 8, 8), slice(None)), lanes[rows:]))
+    return stores
+
+
+def own_rows(ref, at, rows, shift):
+    return jnp.concatenate([ref[at, h, pl.ds(8 + shift, rows), :] for h in range(ref.shape[1])], 1)
+
+
+def halo_rows(ref, at, rows, shift):
+    start = 8 + rows + shift if shift < 0 else shift
+    return jnp.concatenate([ref[at, h, pl.ds(start, 8), :] for h in range(ref.shape[1])], 1)
+
+
 def backward(
     smooth, lit_b, cz_b, cy_b, cx_b, fac_b, gain_b, ramp_b, image_v,
     image_out, grad_out,
-    ay_b, qz_b, full_b, total, sems,
+    ay_b, qz_b, qy_b, full_b, total, sems,
 ):
     slab, rows, cols = total.shape
     ext = rows + 2 * HALO
@@ -377,43 +438,45 @@
     def rx(value, shift):
         return pltpu.roll(value, shift % cols, 1)
 
-    def ry(value, shift):
-        return pltpu.roll(value, shift % ext, 0)
-
     image_copy = pltpu.make_async_copy(image_v, image_out, sems.at[PARTS])
     image_copy.start()
-    ramp = [ramp_b[i] for i in range(4)]
-    ramp2 = 2.0 * ramp[2]
-    ramp3 = 3.0 * ramp[3]
-
-    def pull(k, rest, down=False):
-        here = smooth[k + 3]
-        lit = lit_b[k + 2]
-        value = ramp[0] + here * (ramp[1] + here * (ramp[2] + here * ramp[3]))
-        deriv = ramp[1] + here * (ramp2 + here * ramp3)
-        shown = lit * value
-        if down:
-            rest = rest + shown
-        direct = lit * deriv + (gain_b[k + 2] * value - rest * fac_b[k + 2])
-        qx = value * cx_b[k + 2]
-        qy = value * cy_b[k + 2]
-        stores = [
-            (ay_b, k + 2, (ry(qy, 1) - ry(qy, -1)) + (direct + rx(qx, 1) - rx(qx, -1))),
-            (qz_b, k + 2, value * cz_b[k + 2]),
-        ]
-        return rest if down else rest - shown, stores
-
-    def pull_down(k, rest):
-        return pull(k, rest, True)
+    def puller(y, down=False):
+        tile_rows = pl.ds(y, 8)
+        ramp = [ramp_b[i, tile_rows, :] for i in range(4)]
+        ramp2 = 2.0 * ramp[2]
+        ramp3 = 3.0 * ramp[3]
+        places = [8 + y] if y < rows else [0, 8 + y]
+
+        def pull(k, rest):
+            cell = (k + 2, tile_rows, slice(None))
+            here = smooth[k + 3, tile_rows, :]
+            lit = lit_b[cell]
+            value = ramp[0] + here * (ramp[1] + here * (ramp[2] + here * ramp[3]))
+            deriv = ramp[1] + here * (ramp2 + here * ramp3)
+            shown = lit * value
+            if down:
+                rest = rest + shown
+            direct = lit * deriv + (gain_b[cell] * value - rest * fac_b[cell])
+            qx = value * cx_b[cell]
+            qy = value * cy_b[cell]
+            stores = [(ay_b, cell, direct + rx(qx, 1) - rx(qx, -1)), (qz_b, cell, value * cz_b[cell])]
+            for h in range(cols // 128):
+                for place in places:
+                    stores.append((qy_b, (k + 2, h, pl.ds(place, 8), slice(None)), qy[:, 128 * h : 128 * h + 128]))
+            return rest if down else rest - shown, stores
+
+        return pull
 
     def gather(k, carry):
-        return carry, [(full_b, k + 1, ay_b[k + 2] + qz_b[k + 1] - qz_b[k + 3])]
+        part = ay_b[k + 2] + qz_b[k + 1] - qz_b[k + 3]
+        own = own_rows(qy_b, k + 2, rows, -1) - own_rows(qy_b, k + 2, rows, 1)
+        halo = halo_rows(qy_b, k + 2, rows, -1) - halo_rows(qy_b, k + 2, rows, 1)
+        return carry, lay(full_b, k + 1, part + jnp.concatenate([own, halo], 0))
 
     def spread(k, carry):
-        here = full_b[k + 1]
-        mid = here[:rows]
-        around = 2.0 * mid + full_b[k, pl.ds(0, rows), :] + full_b[k + 2, pl.ds(0, rows), :]
-        around = around + (ry(here, 1) + ry(here, -1))[:rows] + (rx(mid, 1) + rx(mid, -1))
+        mid = own_rows(full_b, k + 1, rows, 0)
+        around = 2.0 * mid + own_rows(full_b, k, rows, 0) + own_rows(full_b, k + 2, rows, 0)
+        around = around + (own_rows(full_b, k + 1, rows, -1) + own_rows(full_b, k + 1, rows, 1)) + (rx(mid, 1) + rx(mid, -1))
         return carry, [(total, first + sign * k, around)]
 
     outs = []
@@ -424,18 +487,21 @@
         out.start()
         outs.append(out)
 
-    rest = ramp_b[4]
-    grouped((-1, -2), 2, pull_down, rest)
+    rests = {y: ramp_b[4, pl.ds(y, 8), :] for y in range(0, ext, 8)}
+    for y, rest in rests.items():
+        grouped((-1, -2), 2, puller(y, True), rest)
     qz_b[slab + 2] = jnp.zeros((ext, cols), jnp.float32)
     done = 0
     for i in range(PARTS):
         last = i == PARTS - 1
         reach = slab if last else step * (i + 1) + 2
-        rest = grouped(range(done, reach), 2, pull, rest)
+        for y in rests:
+            rests[y] = grouped(range(done, reach), 4, puller(y), rests[y])
         grouped(range(done - 1, slab if last else reach - 1), 4, gather, 0)
         done = reach
         if last:
-            full_b[slab + 1] = qz_b[slab + 1]
+            for ref, index, value in lay(full_b, slab + 1, qz_b[slab + 1]):
+                ref[index] = value
         grouped(range(step * i, step * (i + 1)), 4, spread, 0)
         write(i)
     image_copy.wait()
@@ -496,7 +562,8 @@
             scratch_shapes=[
                 pltpu.VMEM(cells, f32),
                 pltpu.VMEM((slab + 3, ext, cols), f32),
-                pltpu.VMEM((slab + 2, ext, cols), f32),
+                pltpu.VMEM((slab + 2, cols // 128, rows + 16, 128), f32),
+                pltpu.VMEM((slab + 2, cols // 128, rows + 16, 128), f32),
                 pltpu.VMEM(density.shape, f32),
                 pltpu.SemaphoreType.DMA((PARTS + 1,)),
             ],

time: 17.7 us -> 17.4 us (0.983)
  Pallas kernels: 16.9 us -> 16.6 us
    pallas_call x1, Pallas kernels: 15 us -> 14.8 us  [shards(): pl.pallas_call(functools.partial(forward, tiles, slab, rows, cols, 2 * sl...]
where the time goes in v6:
time: 17.4 us; the launch traced here: 17.2 us
  Pallas kernels  16.6 us (95%)
  between operations  0.64 us (4%)
    pallas_call x1, Pallas kernels, shards(): pl.pallas_call(functools.partial(forward, tiles, slab, rows, cols, 2 * sl...  14.8 us
    pallas_call x1, Pallas kernels, shards(): pl.pallas_call(backward, out_shape=(jax.ShapeDtypeStruct((3, rows // 2, c...  1.76 us

profile of v6, /device:TPU:1, one launch (start us, length us, event | category | flops | bytes accessed | tf_op | source)
XLA Modules:
  0.0 17.2 jit_solution(6553067336657953593)
XLA Ops:
  0.6 14.8 %shard_map.86 = (f32[36,24,256]{2,1,0:T(8,128)S(1)}, f32[34,24,256]{2,1,0:T(8,128)S(1)}, f32[34,24,256]{2,1,0:T(8,128)S(1)}, f32[34,24,256]{2,1,0:T(8,128)S(1)},...) custom-call(f32[32,16,256]{2,1,0:T(8,128)} %density.1, ...), custom_call_target="tpu_custom_call" | custom-call | tf_op jit(solution)/shard_map/pallas_call | solution.py:542
  15.5 1.8 %shard_map.87 = (f32[3,8,256]{2,1,0:T(8,128)}, f32[32,16,256]{2,1,0:T(8,128)}) custom-call(f32[36,24,256]{2,1,0:T(8,128)S(1)} %get-tuple-element.11.smooth, f32[34,24,256]{2,1,0:T(8,128)S(1)} %get-tuple-element.12.lit_b, f32[34,24,256]{2,1,0:T(8,128)S(1)} %get-tuple-element.13.cz_b, f32[34,24,256]{2,1,0:T(8,128)S(1)} %get-tuple-element.14.cy_b, ...), custom_call_target="tpu_custom_call" | custom-call | tf_op jit(solution)/shard_map/pallas_call | solution.py:557

commit v7 on v6

--- a/solution.py
+++ b/solution.py
@@ -10,7 +10,7 @@
 
 MESH = pl.DeviceIdType.MESH
 LOG2E = math.log2(math.e)
-CUTS = (0, 8, 14, 20, 26, 32)
+CUTS = (0, 4, 10, 16, 22, 28, 32)
 CHUNKS = len(CUTS) - 1
 PARTS = 4
 HALO = 4
@@ -110,14 +110,6 @@
         for n in range(5):
             info[n, pl.ds(at, HALO), :] = jnp.zeros((HALO, cols), jnp.float32)
 
-    @pl.when(jnp.logical_not(has_prev))
-    def _():
-        clear_rows(rows + HALO)
-
-    @pl.when(jnp.logical_not(has_next))
-    def _():
-        clear_rows(rows)
-
     pl.semaphore_wait(barrier, 1 + has_prev.astype(jnp.int32) + has_next.astype(jnp.int32))
 
     def across(src, dst, n):
@@ -182,6 +174,14 @@
     face.start()
     for i in range(1, CHUNKS - 2):
         halo_start(i)
+
+    @pl.when(jnp.logical_not(has_prev))
+    def _():
+        clear_rows(rows + HALO)
+
+    @pl.when(jnp.logical_not(has_next))
+    def _():
+        clear_rows(rows)
 
     for copy in smalls:
         copy.wait()

time: 17.4 us -> 17.4 us (level)
  no operation moved by 1% of the time
where the time goes in v7:
time: 17.4 us; the launch traced here: 17.3 us
  Pallas kernels  16.6 us (95%)
  between operations  0.64 us (4%)
    pallas_call x1, Pallas kernels, shards(): pl.pallas_call(functools.partial(forward, tiles, slab, rows, cols, 2 * sl...  14.9 us
    pallas_call x1, Pallas kernels, shards(): pl.pallas_call(backward, out_shape=(jax.ShapeDtypeStruct((3, rows // 2, c...  1.76 us

profile of v7, /device:TPU:1, one launch (start us, length us, event | category | flops | bytes accessed | tf_op | source)
XLA Modules:
  0.0 17.3 jit_solution(16773348051304169024)
XLA Ops:
  0.6 14.9 %shard_map.86 = (f32[36,24,256]{2,1,0:T(8,128)S(1)}, f32[34,24,256]{2,1,0:T(8,128)S(1)}, f32[34,24,256]{2,1,0:T(8,128)S(1)}, f32[34,24,256]{2,1,0:T(8,128)S(1)},...) custom-call(f32[32,16,256]{2,1,0:T(8,128)} %density.1, ...), custom_call_target="tpu_custom_call" | custom-call | tf_op jit(solution)/shard_map/pallas_call | solution.py:542
  15.5 1.8 %shard_map.87 = (f32[3,8,256]{2,1,0:T(8,128)}, f32[32,16,256]{2,1,0:T(8,128)}) custom-call(f32[36,24,256]{2,1,0:T(8,128)S(1)} %get-tuple-element.11.smooth, f32[34,24,256]{2,1,0:T(8,128)S(1)} %get-tuple-element.12.lit_b, f32[34,24,256]{2,1,0:T(8,128)S(1)} %get-tuple-element.13.cz_b, f32[34,24,256]{2,1,0:T(8,128)S(1)} %get-tuple-element.14.cy_b, ...), custom_call_target="tpu_custom_call" | custom-call | tf_op jit(solution)/shard_map/pallas_call | solution.py:557
